TPU v7x, 1024 devices: a whole 8x8x8 slice. The times are simulated.
1024 devices in a mesh: row: 8 (over x), col: 128 (over y, z, core).
Axes of the slice: x: 8, y: 8, z: 8, core: 2. Of those that a mesh axis runs over, the one named last changes fastest.
Arguments:
- momentum: float32 [10240, 26624], P('row', 'col'), may hold values from -60 to 60, as said below
- grad: bfloat16 [10240, 26624], P('row', 'col'), may hold values from -6 to 6
- right_prev: float32 [26624, 128], P('col'), may hold values from -6 to 6
Outputs:
- new_momentum: float32 [10240, 26624], P('row', 'col')
- left_factor: float32 [10240, 128], P('row')
- right_next: float32 [26624, 128], P('col')
Inputs may be any that keep to these rules, and one draw needn't show every extreme that they name: `momentum`: columns and rows have scales that differ.
All inputs are finite; a program needn't handle non-finite values.
Results may differ from a plain program's by a relative error of at most 0.0003.
Values sent between devices are 32-bit elements; how exact they have to be, the bound alone decides.
No kernel may reach another device: no remote copies, remote signals or barrier semaphores. Data moves between devices by JAX's collectives and lax.ppermute only.
A program may use at most 32 MiB of HBM per device.

v0:
```python
import jax
import jax.numpy as jnp
from jax import lax
from jax.sharding import PartitionSpec as P

D = 10240
FF = 26624


feedback = 0.05
eps = 1e-06
high = lax.Precision.HIGHEST


def orthonormal(proj, gram):
    lower = jnp.linalg.cholesky(gram)
    return lax.linalg.triangular_solve(lower, proj, left_side=False, lower=True, transpose_a=True)


def per_device(momentum, grad, right_prev):
    buffer = momentum + grad.astype(jnp.float32)
    partial_value = jnp.dot(buffer, right_prev, precision=high, preferred_element_type=jnp.float32)
    proj = lax.psum(partial_value, "col")
    gram = lax.psum(
        jnp.dot(proj.T, proj, precision=high, preferred_element_type=jnp.float32), "row"
    )
    basis = orthonormal(proj, gram)
    partial_back = lax.dot_general(
        buffer, basis, (((0,), (0,)), ((), ())), precision=high, preferred_element_type=jnp.float32
    )
    back = lax.psum(partial_back, "row")
    squares = lax.psum(jnp.sum(back * back, axis=0), "col")
    right_next = back * lax.rsqrt(squares / FF + eps)
    new_momentum = buffer - feedback * jnp.dot(
        basis, back.T, precision=high, preferred_element_type=jnp.float32
    )
    left_factor = basis * jnp.sqrt(jnp.float32(D))
    return (new_momentum, left_factor, right_next)


def solution(mesh):
    return jax.shard_map(
        per_device,
        mesh=mesh,
        in_specs=(P("row", "col"), P("row", "col"), P("col", None)),
        out_specs=(P("row", "col"), P("row", None), P("col", None)),
        check_vma=False,
    )
```

profile of v0, /device:TPU:1, one launch (start us, length us, event | category | flops | bytes accessed | tf_op | source)
XLA Modules:
  0.0 685.8 jit_solution(18415057808137315644)
XLA Ops:
  7.2 0.0 copy-start
  7.2 0.0 all-reduce.4.cloned.1.call-start
  7.2 0.8 copy-done
  8.1 4.4 fusion.2
  12.5 0.0 all-reduce.4.cloned.1.call-update
  12.5 0.0 all-reduce.6.cloned.1.call-start
  12.6 219.5 %all-reduce.4.cloned.1.call-done = f32[1280,128]{1,0:T(8,128)} async-done(((f32[1280,128]{1,0:T(8,128)}), f32[1280,128]{1,0:T(8,128)}) %all-reduce.4.cloned.1.call-update) | async-done | bytes 655376 | tf_op jit(solution)/shard_map/psum | solution.py:23
  232.1 0.0 copy-start.2
  232.1 3.2 fusion.7
  235.3 0.0 all-reduce.6.cloned.1.call-update
  235.3 0.0 all-reduce.8.cloned.1.call-start
  235.4 74.5 %all-reduce.6.cloned.1.call-done = f32[128,128]{0,1:T(8,128)} async-done(((f32[128,128]{0,1:T(8,128)}), f32[128,128]{0,1:T(8,128)}) %all-reduce.6.cloned.1.call-update) | async-done | bytes 65552 | tf_op jit(solution)/shard_map/psum | solution.py:24
  309.8 0.9 copy.7
  310.8 0.9 fusion.6
  311.6 11.7 %cholesky.16 = f32[128,128]{1,0:T(8,128)S(1)} custom-call(f32[128,128]{1,0:T(8,128)S(1)} %fusion.6), custom_call_target="Cholesky" | custom-call | tf_op jit(solution)/shard_map/jit(cholesky)/cholesky | solution.py:16
  323.4 0.6 compare_reduce_fusion
  324.0 0.0 copy-start.1
  324.0 0.0 copy-start.3
  324.0 0.8 fusion.3
  324.8 9.8 %custom-call.6 = f32[1,128,128]{1,2,0:T(8,128)S(1)} custom-call(f32[1,128,128]{2,1,0:T(8,128)S(1)} %fusion.3), custom_call_target="InvertDiagBlocksLowerTriangular" | custom-call | tf_op jit(solution)/shard_map/triangular_solve | solution.py:17
  334.6 0.0 copy-done.2
  334.6 1.5 broadcast_multiply_fusion
  336.1 0.0 copy-done.1
  336.1 0.0 copy-done.3
  336.1 1.7 fusion.1
  337.8 0.0 all-reduce.8.cloned.1.call-update
  337.8 82.4 %all-reduce.8.cloned.1.call-done = f32[208,128]{1,0:T(8,128)} async-done(((f32[208,128]{1,0:T(8,128)}), f32[208,128]{1,0:T(8,128)}) %all-reduce.8.cloned.1.call-update) | async-done | bytes 106512 | tf_op jit(solution)/shard_map/psum | solution.py:31
  420.3 0.9 multiply_reduce_fusion
  421.2 254.4 %psum.31 = f32[128]{0:T(128)S(1)} all-reduce(f32[128]{0:T(128)S(1)} %multiply_reduce_fusion), channel_id=1, replica_groups=mesh['row'=8,'col'=128] {'col'}, use_global_device_ids=true, to_apply=%region_6.7 | all-reduce | flops 128 | bytes 1024 | tf_op jit(solution)/shard_map/psum | solution.py:32
  675.6 0.0 copy-start.4
  675.6 3.0 fusion
  678.6 0.0 copy-done.4
  678.6 0.7 broadcast_multiply_fusion.1
  (2 shorter events, 0.0 us)
Async XLA Ops:
  7.2 0.9 copy-start
  7.2 224.9 %all-reduce.4.cloned.1.call-start = ((), (), s32[]{:S(2)}) async-start(), calls=%async_computation | async-start | bytes 1310720 | tf_op jit(solution)/shard_map/psum | solution.py:23
  12.5 297.3 %all-reduce.6.cloned.1.call-start = ((), (), s32[]{:S(2)}) async-start(), calls=%async_computation.1 | async-start | bytes 131072 | tf_op jit(solution)/shard_map/psum | solution.py:24
  232.1 102.5 %copy-start.2 = (f32[1280,128]{1,0:T(8,128)S(1)}, f32[1280,128]{1,0:T(8,128)}, u32[]{:S(2)}) copy-start(f32[1280,128]{1,0:T(8,128)} %all-reduce.4.cloned.1.call-done) | copy-start | bytes 1966084
  235.3 184.9 %all-reduce.8.cloned.1.call-start = ((), (), s32[]{:S(2)}) async-start(), calls=%async_computation.2 | async-start | bytes 212992 | tf_op jit(solution)/shard_map/psum | solution.py:31
  324.0 12.1 %copy-start.1 = (f32[1280,208]{0,1:T(8,128)S(1)}, f32[1280,208]{0,1:T(8,128)}, u32[]{:S(2)}) copy-start(f32[1280,208]{0,1:T(8,128)} %param.3) | copy-start | bytes 3194884
  324.0 12.1 %copy-start.3 = (bf16[1280,208]{0,1:T(8,128)(2,1)S(1)}, bf16[1280,208]{0,1:T(8,128)(2,1)}, u32[]{:S(2)}) copy-start(bf16[1280,208]{0,1:T(8,128)(2,1)} %param.4) | copy-start | bytes 1597444
  675.6 3.0 copy-start.4
Sparse Core Ops, SparseCore 0:
  12.6 219.4 all-reduce.3
  235.4 74.3 all-reduce.5
  338.0 82.2 all-reduce.7
where the time goes:
time: 686 us
  waiting for transfers between devices  376 us (55%)
  blocking collectives  254 us (37%)
  other arithmetic  25.4 us (4%)
  matrix products  13.8 us (2%)
  between operations  13.8 us (2%)
    psum x1, blocking collectives, per_device(): squares = lax.psum(jnp.sum(back * back, axis=0), 'col')  254 us
    psum x1, waiting for transfers between devices, per_device(): proj = lax.psum(partial_value, 'col')  220 us
    psum x1, waiting for transfers between devices, per_device(): back = lax.psum(partial_back, 'row')  82.4 us
    psum x1, waiting for transfers between devices, per_device(): lax.psum(jnp.dot(proj.T, proj, precision=high, preferred_element_type=jnp...  74.5 us
  transfers between devices with their start and end apart: 3, of which 3 were waited for; matrix products, arithmetic and copies ran while one was open for 0% of the time, Pallas kernels for 0%

commit v1 on v0

v1 whole, which is shorter than its diff:
```python
import jax
import jax.numpy as jnp
from jax import lax
from jax.sharding import Mesh, PartitionSpec as P

D = 10240
FF = 26624
RANK = 128

feedback = 0.05
eps = 1e-06
high = lax.Precision.HIGHEST
col = ("y", "z", "core")


def mm(a, b, dims):
    return lax.dot_general(a, b, (dims, ((), ())), precision=high, preferred_element_type=jnp.float32)


def exchange(parts, axis):
    return lax.all_to_all(parts, axis, 0, 0)


def copies(x, n):
    return jnp.broadcast_to(x[None], (n,) + x.shape)


def sum_over_col(partial):
    rows = partial.shape[0]
    half = jnp.sum(exchange(partial.reshape(2, rows // 2, RANK), "core"), axis=0)
    share = jnp.sum(exchange(half.reshape(8, rows // 16, RANK), "y"), axis=0)
    share = jnp.sum(exchange(copies(share, 8), "z"), axis=0)
    half = exchange(copies(share, 8), "y").reshape(rows // 2, RANK)
    return lax.all_gather(half, "core", axis=0, tiled=True)


def sum_over_row(partial):
    rows, width = partial.shape
    share = jnp.sum(exchange(partial.reshape(8, rows // 8, width), "row"), axis=0)
    return exchange(copies(share, 8), "row").reshape(rows, width)


def sum_small(x):
    x = lax.psum(x, "core")
    x = jnp.sum(exchange(copies(x, 8), "y"), axis=0)
    return jnp.sum(exchange(copies(x, 8), "z"), axis=0)


def per_device(momentum, grad, right_prev):
    buffer = momentum + grad.astype(jnp.float32)
    proj = sum_over_col(mm(buffer, right_prev, ((1,), (0,))))
    products = jnp.concatenate(
        [mm(proj, proj, ((0,), (0,))), mm(proj, buffer, ((0,), (0,)))], axis=1
    )
    products = sum_over_row(products)
    gram, raw = products[:, :RANK], products[:, RANK:]
    lower = jnp.linalg.cholesky(gram)
    inverse = lax.linalg.triangular_solve(
        lower, jnp.eye(RANK, dtype=jnp.float32), left_side=True, lower=True
    )
    back = mm(raw, inverse, ((0,), (1,)))
    basis = mm(proj, inverse, ((1,), (1,)))
    squares = sum_small(jnp.sum((back * back).reshape(-1, 8, RANK), axis=0))
    squares = jnp.sum(squares, axis=0, keepdims=True)
    right_next = back * lax.rsqrt(squares / FF + eps)
    new_momentum = buffer - feedback * mm(basis, back, ((1,), (1,)))
    left_factor = basis * jnp.sqrt(jnp.float32(D))
    return (new_momentum, left_factor, right_next)


def solution(mesh):
    fine = Mesh(mesh.devices.reshape(8, 8, 8, 2), ("row", "y", "z", "core"))
    return jax.shard_map(
        per_device,
        mesh=fine,
        in_specs=(P("row", col), P("row", col), P(col, None)),
        out_specs=(P("row", col), P("row", None), P(col, None)),
        check_vma=False,
    )
```

time: 686 us -> 158 us (0.23)
  waiting for transfers between devices: 376 us -> 10.1 us
  blocking collectives: 254 us -> 103 us
  between operations: 13.8 us -> 0.78 us
    psum x3 -> x0, waiting for transfers between devices: 376 us -> none  [the longest x1 220 us: per_device(): proj = lax.psum(partial_value, 'col')]
    psum x1, blocking collectives: 254 us -> 4.91 us  [sum_small(): x = lax.psum(x, 'core')]
    all_to_all x0 -> x6, blocking collectives: none -> 91.9 us  [exchange(): return lax.all_to_all(parts, axis, 0, 0)]
    all_to_all x0 -> x2, waiting for transfers between devices: none -> 10.1 us  [exchange(): return lax.all_to_all(parts, axis, 0, 0)]
  transfers between devices with their start and end apart: 3 -> 2, of which waited for: 3 -> 2; matrix products, arithmetic and copies ran while one was open for 0% -> 2% of each run, Pallas kernels for 0% -> 0%
where the time goes in v1:
time: 158 us; the launch traced here: 157 us
  blocking collectives  103 us (65%)
  other arithmetic  23.7 us (15%)
  waiting for transfers between devices  10.1 us (6%)
  matrix products  10 us (6%)
  starting transfers between devices  6.68 us (4%)
  local copies, waits for them, and re-layouts  2.43 us (2%)
    all_to_all x6, blocking collectives, exchange(): return lax.all_to_all(parts, axis, 0, 0)  91.9 us
    another operation x3, other arithmetic, per_device(): lower = jnp.linalg.cholesky(gram)  12.4 us
    another operation x2, other arithmetic, per_device(): lax.linalg.triangular_solve(lower, jnp.eye(RANK, dtype=jnp.float32), left...  10.5 us
    all_to_all x2, waiting for transfers between devices, exchange(): return lax.all_to_all(parts, axis, 0, 0)  10.1 us
    dot_general x6, matrix products, mm(): lax.dot_general(a, b, (dims, ((), ())), precision=high, preferred_element...  9.78 us
    all_to_all x2, starting transfers between devices, exchange(): return lax.all_to_all(parts, axis, 0, 0)  6.68 us
    all_gather x1, blocking collectives, sum_over_col(): return lax.all_gather(half, 'core', axis=0, tiled=True)  6.5 us
    psum x1, blocking collectives, sum_small(): x = lax.psum(x, 'core')  4.91 us
  transfers between devices with their start and end apart: 2, of which 2 were waited for; matrix products, arithmetic and copies ran while one was open for 2% of the time, Pallas kernels for 0%

profile of v1, /device:TPU:1, one launch (start us, length us, event | category | flops | bytes accessed | tf_op | source)
XLA Modules:
  0.0 156.9 jit_solution(17530883616776317104)
XLA Ops:
  0.6 0.0 copy-start
  0.6 0.9 copy-done
  1.5 3.6 %fusion.2 = f32[1280,128]{1,0:T(8,128)S(1)} fusion(f32[208,128]{1,0:T(8,128)S(1)} %copy-done, f32[1280,208]{0,1:T(8,128)} %param.3, bf16[1280,208]{0,1:T(8,128)(2,1)} %param.4), kind=kOutput, calls=%fused_computation.4 | convolution fusion | flops 409477120 | bytes 2359296 | tf_op jit(solution)/shard_map/dot_general | solution.py:17
  5.1 18.0 %all_to_all.40 = f32[2,640,128]{2,1,0:T(8,128)S(1)} all-to-all(f32[2,640,128]{2,1,0:T(8,128)S(1)} %bitcast.25), channel_id=1, replica_groups=mesh['row'=8,'y'=8,'z'=8,'core'=2] {'core'}, dimensions={0} | all-to-all | bytes 1310720 | tf_op jit(solution)/shard_map/all_to_all | solution.py:21
  23.2 16.1 %all_to_all.41 = f32[8,80,128]{2,1,0:T(8,128)S(1)} all-to-all(f32[8,80,128]{2,1,0:T(8,128)S(1)} %bitcast.26), channel_id=1, replica_groups=mesh['row'=8,'y'=8,'z'=8,'core'=2] {'y'}, dimensions={0} | all-to-all | bytes 655360 | tf_op jit(solution)/shard_map/all_to_all | solution.py:21
  39.4 18.0 %all_to_all.42 = f32[8,80,128]{2,1,0:T(8,128)S(1)} all-to-all(f32[8,80,128]{2,1,0:T(8,128)S(1)} %broadcast_in_dim.11), channel_id=1, replica_groups=mesh['row'=8,'y'=8,'z'=8,'core'=2] {'z'}, dimensions={0} | all-to-all | bytes 655360 | tf_op jit(solution)/shard_map/all_to_all | solution.py:21
  57.4 0.0 copy-start.1
  57.5 0.0 copy-start.2
  57.5 12.6 %all_to_all.43 = f32[8,80,128]{2,1,0:T(8,128)S(1)} all-to-all(f32[8,80,128]{2,1,0:T(8,128)S(1)} %broadcast_in_dim.12), channel_id=1, replica_groups=mesh['row'=8,'y'=8,'z'=8,'core'=2] {'y'}, dimensions={0} | all-to-all | bytes 655360 | tf_op jit(solution)/shard_map/all_to_all | solution.py:21
  70.1 6.5 %all_gather.3 = f32[1280,128]{1,0:T(8,128)S(1)} all-gather(f32[640,128]{1,0:T(8,128)S(1)} %bitcast.27), channel_id=1, replica_groups=mesh['row'=8,'y'=8,'z'=8,'core'=2] {'core'}, dimensions={0}, use_global_device_ids=true | all-gather | bytes 983040 | tf_op jit(solution)/shard_map/all_gather | solution.py:34
  76.6 0.0 copy-done.1
  76.6 0.0 copy-done.2
  76.6 1.0 fusion.1
  77.6 1.2 fusion.9
  78.8 0.1 copy.10
  79.0 15.7 %all_to_all.44 = f32[8,16,336]{2,1,0:T(8,128)S(1)} all-to-all(f32[8,16,336]{2,1,0:T(8,128)S(1)} %bitcast.31), channel_id=1, replica_groups=mesh['row'=8,'y'=8,'z'=8,'core'=2] {'row'}, dimensions={0} | all-to-all | bytes 344064 | tf_op jit(solution)/shard_map/all_to_all | solution.py:21
  94.7 11.4 %all_to_all.45 = f32[8,16,336]{2,1,0:T(8,128)S(1)} all-to-all(f32[8,16,336]{2,1,0:T(8,128)S(1)} %broadcast_in_dim.14), channel_id=1, replica_groups=mesh['row'=8,'y'=8,'z'=8,'core'=2] {'row'}, dimensions={0} | all-to-all | bytes 344064 | tf_op jit(solution)/shard_map/all_to_all | solution.py:21
  106.1 0.1 copy.13
  106.2 11.7 %cholesky.17 = f32[128,128]{1,0:T(8,128)S(1)} custom-call(f32[128,128]{1,0:T(8,128)S(1)} %fusion.8), custom_call_target="Cholesky" | custom-call | tf_op jit(solution)/shard_map/jit(cholesky)/cholesky | solution.py:57
  118.0 0.6 compare_reduce_fusion
  118.6 0.7 fusion.5
  119.3 9.8 %custom-call.6 = f32[1,128,128]{1,2,0:T(8,128)S(1)} custom-call(f32[1,128,128]{2,1,0:T(8,128)S(1)} %fusion.5), custom_call_target="InvertDiagBlocksLowerTriangular" | custom-call | tf_op jit(solution)/shard_map/triangular_solve | solution.py:58
  129.1 0.2 fusion.6
  129.4 0.4 bitcast_reduce_fusion
  129.7 4.9 %psum.7 = f32[8,128]{1,0:T(8,128)S(1)} all-reduce(f32[8,128]{1,0:T(8,128)S(1)} %get-tuple-element.5), channel_id=1, replica_groups=mesh['row'=8,'y'=8,'z'=8,'core'=2] {'core'}, use_global_device_ids=true, to_apply=%region_7.8 | all-reduce | flops 1024 | bytes 8192 | tf_op jit(solution)/shard_map/psum | solution.py:44
  134.7 0.6 broadcast_in_dim.15
  135.3 3.3 %all-to-all-start.6 = ((f32[8,8,128]{2,1,0:T(8,128)}), f32[8,8,128]{2,1,0:T(8,128)S(1)}, u32[]{:S(2)}, u32[]{:S(2)}) async-start(f32[8,8,128]{2,1,0:T(8,128)} %broadcast_in_dim.15), calls=%async_computation.6 | async-start | bytes 65536 | tf_op jit(solution)/shard_map/all_to_all | solution.py:21
  138.6 1.5 broadcast_multiply_fusion
  140.2 5.3 %all-to-all-done.6 = f32[8,8,128]{2,1,0:T(8,128)S(1)} async-done(((f32[8,8,128]{2,1,0:T(8,128)}), f32[8,8,128]{2,1,0:T(8,128)S(1)}, u32[]{:S(2)}, u32[]{:S(2)}) %all-to-all-start.6) | async-done | bytes 32800 | tf_op jit(solution)/shard_map/all_to_all | solution.py:21
  145.4 0.6 broadcast_in_dim.16
  146.1 3.3 %all-to-all-start.7 = ((f32[8,8,128]{2,1,0:T(8,128)}), f32[8,8,128]{2,1,0:T(8,128)S(1)}, u32[]{:S(2)}, u32[]{:S(2)}) async-start(f32[8,8,128]{2,1,0:T(8,128)} %broadcast_in_dim.16), calls=%async_computation.7 | async-start | bytes 65536 | tf_op jit(solution)/shard_map/all_to_all | solution.py:21
  149.4 2.0 %fusion = f32[1280,208]{0,1:T(8,128)} fusion(f32[1280,128]{1,0:T(8,128)S(1)} %get-tuple-element.4, f32[208,128]{1,0:T(8,128)S(1)} %get-tuple-element.6, f32[1280,208]{0,1:T(8,128)S(1)} %copy-done.1, bf16[1280,208]{0,1:T(8,128)(2,1)S(1)} %copy-done.2), kind=kOutput, calls=%fused_computation.1 | convolution fusion | flops 410009600 | bytes 3424256 | tf_op jit(solution)/shard_map/dot_general | solution.py:17
  151.4 4.8 %all-to-all-done.7 = f32[8,8,128]{2,1,0:T(8,128)S(1)} async-done(((f32[8,8,128]{2,1,0:T(8,128)}), f32[8,8,128]{2,1,0:T(8,128)S(1)}, u32[]{:S(2)}, u32[]{:S(2)}) %all-to-all-start.7) | async-done | bytes 32800 | tf_op jit(solution)/shard_map/all_to_all | solution.py:21
  156.3 0.7 broadcast_multiply_fusion.1
  (14 shorter events, 0.3 us)
Async XLA Ops:
  0.6 0.9 copy-start
  57.4 19.1 %copy-start.1 = (f32[1280,208]{0,1:T(8,128)S(1)}, f32[1280,208]{0,1:T(8,128)}, u32[]{:S(2)}) copy-start(f32[1280,208]{0,1:T(8,128)} %param.3) | copy-start | bytes 3194884
  57.5 19.1 %copy-start.2 = (bf16[1280,208]{0,1:T(8,128)(2,1)S(1)}, bf16[1280,208]{0,1:T(8,128)(2,1)}, u32[]{:S(2)}) copy-start(bf16[1280,208]{0,1:T(8,128)(2,1)} %param.4) | copy-start | bytes 1597444
  135.3 10.1 %all-to-all-start.6 = ((f32[8,8,128]{2,1,0:T(8,128)}), f32[8,8,128]{2,1,0:T(8,128)S(1)}, u32[]{:S(2)}, u32[]{:S(2)}) async-start(f32[8,8,128]{2,1,0:T(8,128)} %broadcast_in_dim.15), calls=%async_computation.6 | async-start | bytes 65536 | tf_op jit(solution)/shard_map/all_to_all | solution.py:21
  146.1 10.2 %all-to-all-start.7 = ((f32[8,8,128]{2,1,0:T(8,128)}), f32[8,8,128]{2,1,0:T(8,128)S(1)}, u32[]{:S(2)}, u32[]{:S(2)}) async-start(f32[8,8,128]{2,1,0:T(8,128)} %broadcast_in_dim.16), calls=%async_computation.7 | async-start | bytes 65536 | tf_op jit(solution)/shard_map/all_to_all | solution.py:21

commit v2 on v1

--- a/solution.py
+++ b/solution.py
@@ -1,6 +1,8 @@
 import jax
 import jax.numpy as jnp
 from jax import lax
+from jax.experimental import pallas as pl
+from jax.experimental.pallas import tpu as pltpu
 from jax.sharding import Mesh, PartitionSpec as P
 
 D = 10240
@@ -46,6 +48,59 @@
     return jnp.sum(exchange(copies(x, 8), "z"), axis=0)
 
 
+def factor_inverse(gram_ref, out_ref):
+    tile = (8, RANK)
+    lane = lax.broadcasted_iota(jnp.int32, tile, 1)
+    sub = lax.broadcasted_iota(jnp.int32, tile, 0)
+    rows = [gram_ref[8 * t : 8 * t + 8, :] for t in range(RANK // 8)]
+    for k in range(RANK // 8):
+        first = 8 * k
+        panel = rows[k]
+        inside = (lane >= first) & (lane < first + 8)
+        cols = [jnp.broadcast_to(panel[:, first + q : first + q + 1], tile) for q in range(8)]
+        a = {}
+        for q in range(8):
+            for p in range(q + 1):
+                a[p, q] = jnp.broadcast_to(cols[q][p : p + 1, :], tile)
+        inv, m = [], {}
+        for p in range(8):
+            inv.append(1.0 / a[p, p])
+            for q in range(p + 1, 8):
+                m[q, p] = a[p, q] * inv[p]
+            for q in range(p + 1, 8):
+                for s in range(q, 8):
+                    a[q, s] = a[q, s] - m[q, p] * a[p, s]
+        start = jnp.where(inside, (lane - first == sub).astype(jnp.float32), panel)
+        r = []
+        for i in range(8):
+            row = jnp.broadcast_to(start[i : i + 1, :], tile)
+            for p in range(i):
+                row = row - m[i, p] * r[p]
+            r.append(row)
+        done = jnp.zeros(tile, jnp.float32)
+        for i in range(8):
+            done = jnp.where(sub == i, r[i] * lax.rsqrt(a[i, i]), done)
+        out_ref[first : first + 8, :] = jnp.where(lane <= first + sub, done, 0.0)
+        for t in range(k + 1, RANK // 8):
+            c = [jnp.broadcast_to(rows[t][:, first + q : first + q + 1], tile) for q in range(8)]
+            row = jnp.where(inside, 0.0, rows[t])
+            for p in range(8):
+                w = c[p] * inv[p]
+                for q in range(p + 1, 8):
+                    c[q] = c[q] - w * a[p, q]
+                row = row - w * r[p]
+            rows[t] = row
+
+
+def inverse_factor(gram):
+    return pl.pallas_call(
+        factor_inverse,
+        out_shape=jax.ShapeDtypeStruct((RANK, RANK), jnp.float32),
+        in_specs=[pl.BlockSpec(memory_space=pltpu.VMEM)],
+        out_specs=pl.BlockSpec(memory_space=pltpu.VMEM),
+    )(gram)
+
+
 def per_device(momentum, grad, right_prev):
     buffer = momentum + grad.astype(jnp.float32)
     proj = sum_over_col(mm(buffer, right_prev, ((1,), (0,))))
@@ -54,10 +109,7 @@
     )
     products = sum_over_row(products)
     gram, raw = products[:, :RANK], products[:, RANK:]
-    lower = jnp.linalg.cholesky(gram)
-    inverse = lax.linalg.triangular_solve(
-        lower, jnp.eye(RANK, dtype=jnp.float32), left_side=True, lower=True
-    )
+    inverse = inverse_factor(gram)
     back = mm(raw, inverse, ((0,), (1,)))
     basis = mm(proj, inverse, ((1,), (1,)))
     squares = sum_small(jnp.sum((back * back).reshape(-1, 8, RANK), axis=0))

time: 158 us -> 142 us (0.90)
  other arithmetic: 23.7 us -> 0.81 us
  Pallas kernels: 0 us -> 5.31 us
    another operation x5 -> x0, other arithmetic: 22.9 us -> none  [the longest x3 12.4 us: per_device(): lower = jnp.linalg.cholesky(gram)]
    pallas_call x0 -> x1, Pallas kernels: none -> 5.31 us  [inverse_factor(): pl.pallas_call(factor_inverse, out_shape=jax.ShapeDtypeStruct((RANK, RANK...]
    dot_general x6, matrix products: 9.78 us -> 11.4 us  [mm(): lax.dot_general(a, b, (dims, ((), ())), precision=high, preferred_element...]
  transfers between devices with their start and end apart: 2 -> 2, of which waited for: 2 -> 2; matrix products, arithmetic and copies ran while one was open for 2% -> 3% of each run, Pallas kernels for 0% -> 0%
where the time goes in v2:
time: 142 us; the launch traced here: 140 us
  blocking collectives  103 us (73%)
  matrix products  11.4 us (8%)
  waiting for transfers between devices  9.21 us (6%)
  starting transfers between devices  6.68 us (5%)
  Pallas kernels  5.31 us (4%)
  local copies, waits for them, and re-layouts  2.97 us (2%)
    all_to_all x6, blocking collectives, exchange(): return lax.all_to_all(parts, axis, 0, 0)  91.8 us
    dot_general x6, matrix products, mm(): lax.dot_general(a, b, (dims, ((), ())), precision=high, preferred_element...  11.4 us
    all_to_all x2, waiting for transfers between devices, exchange(): return lax.all_to_all(parts, axis, 0, 0)  9.21 us
    all_to_all x2, starting transfers between devices, exchange(): return lax.all_to_all(parts, axis, 0, 0)  6.68 us
    all_gather x1, blocking collectives, sum_over_col(): return lax.all_gather(half, 'core', axis=0, tiled=True)  6.5 us
    pallas_call x1, Pallas kernels, inverse_factor(): pl.pallas_call(factor_inverse, out_shape=jax.ShapeDtypeStruct((RANK, RANK...  5.31 us
    psum x1, blocking collectives, sum_small(): x = lax.psum(x, 'core')  4.98 us
  transfers between devices with their start and end apart: 2, of which 2 were waited for; matrix products, arithmetic and copies ran while one was open for 3% of the time, Pallas kernels for 0%

profile of v2, /device:TPU:1, one launch (start us, length us, event | category | flops | bytes accessed | tf_op | source)
XLA Modules:
  0.0 140.4 jit_solution(12785357909080185301)
XLA Ops:
  0.6 0.0 copy-start
  0.6 0.9 copy-done
  1.5 3.6 %fusion.2 = f32[1280,128]{1,0:T(8,128)S(1)} fusion(f32[208,128]{1,0:T(8,128)S(1)} %copy-done, f32[1280,208]{0,1:T(8,128)} %param.3, bf16[1280,208]{0,1:T(8,128)(2,1)} %param.4), kind=kOutput, calls=%fused_computation.4 | convolution fusion | flops 409477120 | bytes 2359296 | tf_op jit(solution)/shard_map/dot_general | solution.py:19
  5.1 18.0 %all_to_all.40 = f32[2,640,128]{2,1,0:T(8,128)S(1)} all-to-all(f32[2,640,128]{2,1,0:T(8,128)S(1)} %bitcast.16), channel_id=1, replica_groups=mesh['row'=8,'y'=8,'z'=8,'core'=2] {'core'}, dimensions={0} | all-to-all | bytes 1310720 | tf_op jit(solution)/shard_map/all_to_all | solution.py:23
  23.2 16.1 %all_to_all.41 = f32[8,80,128]{2,1,0:T(8,128)S(1)} all-to-all(f32[8,80,128]{2,1,0:T(8,128)S(1)} %bitcast.17), channel_id=1, replica_groups=mesh['row'=8,'y'=8,'z'=8,'core'=2] {'y'}, dimensions={0} | all-to-all | bytes 655360 | tf_op jit(solution)/shard_map/all_to_all | solution.py:23
  39.4 18.0 %all_to_all.42 = f32[8,80,128]{2,1,0:T(8,128)S(1)} all-to-all(f32[8,80,128]{2,1,0:T(8,128)S(1)} %broadcast_in_dim.10), channel_id=1, replica_groups=mesh['row'=8,'y'=8,'z'=8,'core'=2] {'z'}, dimensions={0} | all-to-all | bytes 655360 | tf_op jit(solution)/shard_map/all_to_all | solution.py:23
  57.4 0.0 copy-start.1
  57.5 0.0 copy-start.2
  57.5 12.6 %all_to_all.43 = f32[8,80,128]{2,1,0:T(8,128)S(1)} all-to-all(f32[8,80,128]{2,1,0:T(8,128)S(1)} %broadcast_in_dim.11), channel_id=1, replica_groups=mesh['row'=8,'y'=8,'z'=8,'core'=2] {'y'}, dimensions={0} | all-to-all | bytes 655360 | tf_op jit(solution)/shard_map/all_to_all | solution.py:23
  70.1 6.5 %all_gather.3 = f32[1280,128]{1,0:T(8,128)S(1)} all-gather(f32[640,128]{1,0:T(8,128)S(1)} %bitcast.18), channel_id=1, replica_groups=mesh['row'=8,'y'=8,'z'=8,'core'=2] {'core'}, dimensions={0}, use_global_device_ids=true | all-gather | bytes 983040 | tf_op jit(solution)/shard_map/all_gather | solution.py:36
  76.6 0.0 copy-done.1
  76.6 0.0 copy-done.2
  76.6 1.0 fusion.1
  77.6 1.2 fusion.5
  78.8 0.1 copy.7
  79.0 15.7 %all_to_all.44 = f32[8,16,336]{2,1,0:T(8,128)S(1)} all-to-all(f32[8,16,336]{2,1,0:T(8,128)S(1)} %bitcast.21), channel_id=1, replica_groups=mesh['row'=8,'y'=8,'z'=8,'core'=2] {'row'}, dimensions={0} | all-to-all | bytes 344064 | tf_op jit(solution)/shard_map/all_to_all | solution.py:23
  94.7 11.3 %all_to_all.45 = f32[8,16,336]{2,1,0:T(8,128)S(1)} all-to-all(f32[8,16,336]{2,1,0:T(8,128)S(1)} %broadcast_in_dim.12), channel_id=1, replica_groups=mesh['row'=8,'y'=8,'z'=8,'core'=2] {'row'}, dimensions={0} | all-to-all | bytes 344064 | tf_op jit(solution)/shard_map/all_to_all | solution.py:23
  106.0 0.6 slice.8.gram_ref
  106.7 5.3 %shard_map.58 = f32[128,128]{1,0:T(8,128)} custom-call(f32[128,128]{1,0:T(8,128)} %slice.8.gram_ref), custom_call_target="tpu_custom_call" | custom-call | tf_op jit(solution)/shard_map/pallas_call | solution.py:96
  112.0 1.2 bitcast_reduce_fusion
  113.2 5.0 %psum.7 = f32[8,128]{1,0:T(8,128)S(1)} all-reduce(f32[8,128]{1,0:T(8,128)S(1)} %get-tuple-element.5), channel_id=1, replica_groups=mesh['row'=8,'y'=8,'z'=8,'core'=2] {'core'}, use_global_device_ids=true, to_apply=%region_5.0 | all-reduce | flops 1024 | bytes 8192 | tf_op jit(solution)/shard_map/psum | solution.py:46
  118.2 0.6 broadcast_in_dim.13
  118.8 3.3 %all-to-all-start.6 = ((f32[8,8,128]{2,1,0:T(8,128)}), f32[8,8,128]{2,1,0:T(8,128)S(1)}, u32[]{:S(2)}, u32[]{:S(2)}) async-start(f32[8,8,128]{2,1,0:T(8,128)} %broadcast_in_dim.13), calls=%async_computation.6 | async-start | bytes 65536 | tf_op jit(solution)/shard_map/all_to_all | solution.py:23
  122.1 2.4 %broadcast_multiply_fusion = (f32[1280,128]{1,0:T(8,128)}, f32[1280,128]{1,0:T(8,128)S(1)}) fusion(f32[1280,128]{1,0:T(8,128)S(1)} %all_gather.3, f32[128,128]{1,0:T(8,128)} %shard_map.58), kind=kOutput, calls=%fused_computation.5 | convolution fusion | flops 251822080 | bytes 2031616 | tf_op jit(solution)/shard_map/dot_general | solution.py:19
  124.5 4.4 %all-to-all-done.6 = f32[8,8,128]{2,1,0:T(8,128)S(1)} async-done(((f32[8,8,128]{2,1,0:T(8,128)}), f32[8,8,128]{2,1,0:T(8,128)S(1)}, u32[]{:S(2)}, u32[]{:S(2)}) %all-to-all-start.6) | async-done | bytes 32800 | tf_op jit(solution)/shard_map/all_to_all | solution.py:23
  128.9 0.6 broadcast_in_dim.14
  129.6 3.3 %all-to-all-start.7 = ((f32[8,8,128]{2,1,0:T(8,128)}), f32[8,8,128]{2,1,0:T(8,128)S(1)}, u32[]{:S(2)}, u32[]{:S(2)}) async-start(f32[8,8,128]{2,1,0:T(8,128)} %broadcast_in_dim.14), calls=%async_computation.7 | async-start | bytes 65536 | tf_op jit(solution)/shard_map/all_to_all | solution.py:23
  132.9 2.0 %fusion = f32[1280,208]{0,1:T(8,128)} fusion(f32[1280,128]{1,0:T(8,128)S(1)} %get-tuple-element.4, f32[208,128]{1,0:T(8,128)S(1)} %get-tuple-element.6, f32[1280,208]{0,1:T(8,128)S(1)} %copy-done.1, bf16[1280,208]{0,1:T(8,128)(2,1)S(1)} %copy-done.2), kind=kOutput, calls=%fused_computation.1 | convolution fusion | flops 410009600 | bytes 3424256 | tf_op jit(solution)/shard_map/dot_general | solution.py:19
  135.0 4.8 %all-to-all-done.7 = f32[8,8,128]{2,1,0:T(8,128)S(1)} async-done(((f32[8,8,128]{2,1,0:T(8,128)}), f32[8,8,128]{2,1,0:T(8,128)S(1)}, u32[]{:S(2)}, u32[]{:S(2)}) %all-to-all-start.7) | async-done | bytes 32800 | tf_op jit(solution)/shard_map/all_to_all | solution.py:23
  139.8 0.7 broadcast_multiply_fusion.1
  (11 shorter events, 0.2 us)
Async XLA Ops:
  0.6 0.9 copy-start
  57.4 19.1 %copy-start.1 = (f32[1280,208]{0,1:T(8,128)S(1)}, f32[1280,208]{0,1:T(8,128)}, u32[]{:S(2)}) copy-start(f32[1280,208]{0,1:T(8,128)} %param.3) | copy-start | bytes 3194884
  57.5 19.1 %copy-start.2 = (bf16[1280,208]{0,1:T(8,128)(2,1)S(1)}, bf16[1280,208]{0,1:T(8,128)(2,1)}, u32[]{:S(2)}) copy-start(bf16[1280,208]{0,1:T(8,128)(2,1)} %param.4) | copy-start | bytes 1597444
  118.8 10.1 %all-to-all-start.6 = ((f32[8,8,128]{2,1,0:T(8,128)}), f32[8,8,128]{2,1,0:T(8,128)S(1)}, u32[]{:S(2)}, u32[]{:S(2)}) async-start(f32[8,8,128]{2,1,0:T(8,128)} %broadcast_in_dim.13), calls=%async_computation.6 | async-start | bytes 65536 | tf_op jit(solution)/shard_map/all_to_all | solution.py:23
  129.6 10.2 %all-to-all-start.7 = ((f32[8,8,128]{2,1,0:T(8,128)}), f32[8,8,128]{2,1,0:T(8,128)S(1)}, u32[]{:S(2)}, u32[]{:S(2)}) async-start(f32[8,8,128]{2,1,0:T(8,128)} %broadcast_in_dim.14), calls=%async_computation.7 | async-start | bytes 65536 | tf_op jit(solution)/shard_map/all_to_all | solution.py:23

commit v3 on v2

--- a/solution.py
+++ b/solution.py
@@ -42,17 +42,11 @@
     return exchange(copies(share, 8), "row").reshape(rows, width)
 
 
-def sum_small(x):
-    x = lax.psum(x, "core")
-    x = jnp.sum(exchange(copies(x, 8), "y"), axis=0)
-    return jnp.sum(exchange(copies(x, 8), "z"), axis=0)
-
-
-def factor_inverse(gram_ref, out_ref):
+def factor_inverse(products_ref, inverse_ref):
     tile = (8, RANK)
     lane = lax.broadcasted_iota(jnp.int32, tile, 1)
     sub = lax.broadcasted_iota(jnp.int32, tile, 0)
-    rows = [gram_ref[8 * t : 8 * t + 8, :] for t in range(RANK // 8)]
+    rows = [products_ref[8 * t : 8 * t + 8, :RANK] for t in range(RANK // 8)]
     for k in range(RANK // 8):
         first = 8 * k
         panel = rows[k]
@@ -80,7 +74,7 @@
         done = jnp.zeros(tile, jnp.float32)
         for i in range(8):
             done = jnp.where(sub == i, r[i] * lax.rsqrt(a[i, i]), done)
-        out_ref[first : first + 8, :] = jnp.where(lane <= first + sub, done, 0.0)
+        inverse_ref[first : first + 8, :] = jnp.where(lane <= first + sub, done, 0.0)
         for t in range(k + 1, RANK // 8):
             c = [jnp.broadcast_to(rows[t][:, first + q : first + q + 1], tile) for q in range(8)]
             row = jnp.where(inside, 0.0, rows[t])
@@ -92,28 +86,44 @@
             rows[t] = row
 
 
-def inverse_factor(gram):
-    return pl.pallas_call(
-        factor_inverse,
-        out_shape=jax.ShapeDtypeStruct((RANK, RANK), jnp.float32),
-        in_specs=[pl.BlockSpec(memory_space=pltpu.VMEM)],
-        out_specs=pl.BlockSpec(memory_space=pltpu.VMEM),
-    )(gram)
+def back_kernel(products_ref, inverse_ref, back_ref, squares_ref):
+    factor_inverse(products_ref, inverse_ref)
+    back = mm(products_ref[:, RANK:].T, inverse_ref[...], ((1,), (1,)))
+    back_ref[...] = back
+    squares = jnp.sum((back * back).reshape(-1, 8, RANK), axis=0)
+    for i in range(squares_ref.shape[0]):
+        squares_ref[i] = squares
+
+
+def proj_kernel(momentum_ref, grad_ref, right_ref, out_ref):
+    for i in range(out_ref.shape[0] // 256):
+        part = slice(256 * i, 256 * i + 256)
+        buffer = momentum_ref[:, part] + grad_ref[:, part].astype(jnp.float32)
+        out_ref[part, :] = mm(buffer, right_ref[...], ((0,), (0,)))
 
 
 def per_device(momentum, grad, right_prev):
+    rows, width = momentum.shape
+    partial = pl.pallas_call(
+        proj_kernel, out_shape=jax.ShapeDtypeStruct((rows, RANK), jnp.float32)
+    )(momentum.T, grad.T, right_prev)
+    proj = sum_over_col(partial)
     buffer = momentum + grad.astype(jnp.float32)
-    proj = sum_over_col(mm(buffer, right_prev, ((1,), (0,))))
     products = jnp.concatenate(
         [mm(proj, proj, ((0,), (0,))), mm(proj, buffer, ((0,), (0,)))], axis=1
     )
     products = sum_over_row(products)
-    gram, raw = products[:, :RANK], products[:, RANK:]
-    inverse = inverse_factor(gram)
-    back = mm(raw, inverse, ((0,), (1,)))
+    inverse, back, squares = pl.pallas_call(
+        back_kernel,
+        out_shape=(
+            jax.ShapeDtypeStruct((RANK, RANK), jnp.float32),
+            jax.ShapeDtypeStruct((width, RANK), jnp.float32),
+            jax.ShapeDtypeStruct((16, 8, RANK), jnp.float32),
+        ),
+    )(products)
     basis = mm(proj, inverse, ((1,), (1,)))
-    squares = sum_small(jnp.sum((back * back).reshape(-1, 8, RANK), axis=0))
-    squares = jnp.sum(squares, axis=0, keepdims=True)
+    squares = jnp.sum(exchange(squares, ("y", "core")), axis=0)
+    squares = jnp.sum(exchange(copies(squares, 8), "z"), axis=(0, 1))
     right_next = back * lax.rsqrt(squares / FF + eps)
     new_momentum = buffer - feedback * mm(basis, back, ((1,), (1,)))
     left_factor = basis * jnp.sqrt(jnp.float32(D))

time: 142 us -> 139 us (0.979)
  matrix products: 11.4 us -> 6.65 us
  Pallas kernels: 5.31 us -> 9.39 us
  blocking collectives: 103 us -> 99.8 us
  starting transfers between devices: 6.68 us -> 9.65 us
  local copies, waits for them, and re-layouts: 2.97 us -> 0.81 us
    psum x1 -> x0, blocking collectives: 4.98 us -> none  [sum_small(): x = lax.psum(x, 'core')]
    dot_general x6 -> x4, matrix products: 11.4 us -> 6.65 us  [mm(): lax.dot_general(a, b, (dims, ((), ())), precision=high, preferred_element...]
    pallas_call x1 -> x2, Pallas kernels: 5.31 us -> 9.39 us  [the longest x1 5.9 us: per_device(): pl.pallas_call(back_kernel, out_shape=(jax.ShapeDtypeStruct((RANK, RANK),...]
    all_to_all x2, starting transfers between devices: 6.68 us -> 9.65 us  [exchange(): return lax.all_to_all(parts, axis, 0, 0)]
    all_to_all x6, blocking collectives: 91.8 us -> 93.3 us  [exchange(): return lax.all_to_all(parts, axis, 0, 0)]
where the time goes in v3:
time: 139 us; the launch traced here: 138 us
  blocking collectives  99.8 us (72%)
  waiting for transfers between devices  10.2 us (7%)
  starting transfers between devices  9.65 us (7%)
  Pallas kernels  9.39 us (7%)
  matrix products  6.65 us (5%)
    all_to_all x6, blocking collectives, exchange(): return lax.all_to_all(parts, axis, 0, 0)  93.3 us
    all_to_all x2, waiting for transfers between devices, exchange(): return lax.all_to_all(parts, axis, 0, 0)  10.2 us
    all_to_all x2, starting transfers between devices, exchange(): return lax.all_to_all(parts, axis, 0, 0)  9.65 us
    dot_general x4, matrix products, mm(): lax.dot_general(a, b, (dims, ((), ())), precision=high, preferred_element...  6.65 us
    all_gather x1, blocking collectives, sum_over_col(): return lax.all_gather(half, 'core', axis=0, tiled=True)  6.5 us
    pallas_call x1, Pallas kernels, per_device(): pl.pallas_call(back_kernel, out_shape=(jax.ShapeDtypeStruct((RANK, RANK),...  5.9 us
    pallas_call x1, Pallas kernels, per_device(): pl.pallas_call(proj_kernel, out_shape=jax.ShapeDtypeStruct((rows, RANK),...  3.49 us
  transfers between devices with their start and end apart: 2, of which 2 were waited for; matrix products, arithmetic and copies ran while one was open for 3% of the time, Pallas kernels for 0%

profile of v3, /device:TPU:1, one launch (start us, length us, event | category | flops | bytes accessed | tf_op | source)
XLA Modules:
  0.0 138.1 jit_solution(7388913663804333158)
XLA Ops:
  0.6 3.5 %shard_map.58 = f32[1280,128]{1,0:T(8,128)} custom-call(f32[208,1280]{1,0:T(8,128)} %bitcast.14, bf16[208,1280]{1,0:T(8,128)(2,1)} %bitcast.15, f32[208,128]{1,0:T(8,128)} %right_ref.1), custom_call_target="tpu_custom_call" | custom-call | tf_op jit(solution)/shard_map/pallas_call | solution.py:107
  4.1 19.1 %all_to_all.40 = f32[2,640,128]{2,1,0:T(8,128)S(1)} all-to-all(f32[2,640,128]{2,1,0:T(8,128)} %bitcast.16), channel_id=1, replica_groups=mesh['row'=8,'y'=8,'z'=8,'core'=2] {'core'}, dimensions={0} | all-to-all | bytes 1310720 | tf_op jit(solution)/shard_map/all_to_all | solution.py:23
  23.3 16.1 %all_to_all.41 = f32[8,80,128]{2,1,0:T(8,128)S(1)} all-to-all(f32[8,80,128]{2,1,0:T(8,128)S(1)} %bitcast.17), channel_id=1, replica_groups=mesh['row'=8,'y'=8,'z'=8,'core'=2] {'y'}, dimensions={0} | all-to-all | bytes 655360 | tf_op jit(solution)/shard_map/all_to_all | solution.py:23
  39.5 18.0 %all_to_all.42 = f32[8,80,128]{2,1,0:T(8,128)S(1)} all-to-all(f32[8,80,128]{2,1,0:T(8,128)S(1)} %broadcast_in_dim.8), channel_id=1, replica_groups=mesh['row'=8,'y'=8,'z'=8,'core'=2] {'z'}, dimensions={0} | all-to-all | bytes 655360 | tf_op jit(solution)/shard_map/all_to_all | solution.py:23
  57.5 0.0 copy-start
  57.5 0.0 copy-start.1
  57.6 12.6 %all_to_all.43 = f32[8,80,128]{2,1,0:T(8,128)S(1)} all-to-all(f32[8,80,128]{2,1,0:T(8,128)S(1)} %broadcast_in_dim.9), channel_id=1, replica_groups=mesh['row'=8,'y'=8,'z'=8,'core'=2] {'y'}, dimensions={0} | all-to-all | bytes 655360 | tf_op jit(solution)/shard_map/all_to_all | solution.py:23
  70.1 6.5 %all_gather.3 = f32[1280,128]{1,0:T(8,128)S(1)} all-gather(f32[640,128]{1,0:T(8,128)S(1)} %bitcast.18), channel_id=1, replica_groups=mesh['row'=8,'y'=8,'z'=8,'core'=2] {'core'}, dimensions={0}, use_global_device_ids=true | all-gather | bytes 983040 | tf_op jit(solution)/shard_map/all_gather | solution.py:36
  76.6 0.0 copy-done
  76.6 0.0 copy-done.1
  76.6 1.0 fusion.1
  77.7 1.2 fusion.2
  78.9 0.1 copy.7
  79.0 15.7 %all_to_all.44 = f32[8,16,336]{2,1,0:T(8,128)S(1)} all-to-all(f32[8,16,336]{2,1,0:T(8,128)S(1)} %bitcast.20), channel_id=1, replica_groups=mesh['row'=8,'y'=8,'z'=8,'core'=2] {'row'}, dimensions={0} | all-to-all | bytes 344064 | tf_op jit(solution)/shard_map/all_to_all | solution.py:23
  94.8 11.8 %all_to_all.45 = f32[8,16,336]{2,1,0:T(8,128)} all-to-all(f32[8,16,336]{2,1,0:T(8,128)S(1)} %broadcast_in_dim.10), channel_id=1, replica_groups=mesh['row'=8,'y'=8,'z'=8,'core'=2] {'row'}, dimensions={0} | all-to-all | bytes 344064 | tf_op jit(solution)/shard_map/all_to_all | solution.py:23
  106.6 5.9 %shard_map.59 = (f32[128,128]{1,0:T(8,128)}, f32[208,128]{1,0:T(8,128)}, f32[16,8,128]{2,1,0:T(8,128)}) custom-call(f32[128,336]{1,0:T(8,128)} %bitcast.19), custom_call_target="tpu_custom_call" | custom-call | tf_op jit(solution)/shard_map/pallas_call | solution.py:116
  112.5 6.3 %all-to-all-start.6 = ((f32[16,8,128]{2,1,0:T(8,128)}), f32[16,8,128]{2,1,0:T(8,128)S(1)}, u32[]{:S(2)}, u32[]{:S(2)}) async-start(f32[16,8,128]{2,1,0:T(8,128)} %get-tuple-element.8), calls=%async_computation.6 | async-start | bytes 131072 | tf_op jit(solution)/shard_map/all_to_all | solution.py:23
  118.8 0.0 copy-start.2
  118.8 2.4 %broadcast_multiply_fusion = (f32[1280,128]{1,0:T(8,128)}, f32[1280,128]{1,0:T(8,128)S(1)}) fusion(f32[1280,128]{1,0:T(8,128)S(1)} %all_gather.3, f32[128,128]{1,0:T(8,128)} %get-tuple-element.6), kind=kOutput, calls=%fused_computation.4 | convolution fusion | flops 251822080 | bytes 2031616 | tf_op jit(solution)/shard_map/dot_general | solution.py:19
  121.2 5.4 %all-to-all-done.6 = f32[16,8,128]{2,1,0:T(8,128)S(1)} async-done(((f32[16,8,128]{2,1,0:T(8,128)}), f32[16,8,128]{2,1,0:T(8,128)S(1)}, u32[]{:S(2)}, u32[]{:S(2)}) %all-to-all-start.6) | async-done | bytes 65568 | tf_op jit(solution)/shard_map/all_to_all | solution.py:23
  126.7 0.6 broadcast_in_dim.11
  127.3 3.3 %all-to-all-start.7 = ((f32[8,8,128]{2,1,0:T(8,128)}), f32[8,8,128]{2,1,0:T(8,128)S(1)}, u32[]{:S(2)}, u32[]{:S(2)}) async-start(f32[8,8,128]{2,1,0:T(8,128)} %broadcast_in_dim.11), calls=%async_computation.7 | async-start | bytes 65536 | tf_op jit(solution)/shard_map/all_to_all | solution.py:23
  130.6 0.0 copy-done.2
  130.6 2.0 %fusion = f32[1280,208]{0,1:T(8,128)} fusion(f32[1280,128]{1,0:T(8,128)S(1)} %get-tuple-element.10, f32[208,128]{1,0:T(8,128)S(1)} %copy-done.2, f32[1280,208]{0,1:T(8,128)S(1)} %copy-done, bf16[1280,208]{0,1:T(8,128)(2,1)S(1)} %copy-done.1), kind=kOutput, calls=%fused_computation.1 | convolution fusion | flops 410009600 | bytes 3424256 | tf_op jit(solution)/shard_map/dot_general | solution.py:19
  132.6 4.8 %all-to-all-done.7 = f32[8,8,128]{2,1,0:T(8,128)S(1)} async-done(((f32[8,8,128]{2,1,0:T(8,128)}), f32[8,8,128]{2,1,0:T(8,128)S(1)}, u32[]{:S(2)}, u32[]{:S(2)}) %all-to-all-start.7) | async-done | bytes 32800 | tf_op jit(solution)/shard_map/all_to_all | solution.py:23
  137.4 0.7 broadcast_multiply_fusion.1
  (11 shorter events, 0.2 us)
Async XLA Ops:
  57.5 19.1 %copy-start = (f32[1280,208]{0,1:T(8,128)S(1)}, f32[1280,208]{0,1:T(8,128)}, u32[]{:S(2)}) copy-start(f32[1280,208]{0,1:T(8,128)} %param.3) | copy-start | bytes 3194884
  57.5 19.1 %copy-start.1 = (bf16[1280,208]{0,1:T(8,128)(2,1)S(1)}, bf16[1280,208]{0,1:T(8,128)(2,1)}, u32[]{:S(2)}) copy-start(bf16[1280,208]{0,1:T(8,128)(2,1)} %param.4) | copy-start | bytes 1597444
  112.5 14.2 %all-to-all-start.6 = ((f32[16,8,128]{2,1,0:T(8,128)}), f32[16,8,128]{2,1,0:T(8,128)S(1)}, u32[]{:S(2)}, u32[]{:S(2)}) async-start(f32[16,8,128]{2,1,0:T(8,128)} %get-tuple-element.8), calls=%async_computation.6 | async-start | bytes 131072 | tf_op jit(solution)/shard_map/all_to_all | solution.py:23
  118.8 11.8 %copy-start.2 = (f32[208,128]{1,0:T(8,128)S(1)}, f32[208,128]{1,0:T(8,128)}, u32[]{:S(2)}) copy-start(f32[208,128]{1,0:T(8,128)} %get-tuple-element.7) | copy-start | bytes 319492
  127.3 10.2 %all-to-all-start.7 = ((f32[8,8,128]{2,1,0:T(8,128)}), f32[8,8,128]{2,1,0:T(8,128)S(1)}, u32[]{:S(2)}, u32[]{:S(2)}) async-start(f32[8,8,128]{2,1,0:T(8,128)} %broadcast_in_dim.11), calls=%async_computation.7 | async-start | bytes 65536 | tf_op jit(solution)/shard_map/all_to_all | solution.py:23

commit v4 on v3

--- a/solution.py
+++ b/solution.py
@@ -105,7 +105,7 @@
 def per_device(momentum, grad, right_prev):
     rows, width = momentum.shape
     partial = pl.pallas_call(
-        proj_kernel, out_shape=jax.ShapeDtypeStruct((rows, RANK), jnp.float32)
+        proj_kernel, out_shape=pltpu.VMEM((rows, RANK), jnp.float32)
     )(momentum.T, grad.T, right_prev)
     proj = sum_over_col(partial)
     buffer = momentum + grad.astype(jnp.float32)
@@ -116,16 +116,17 @@
     inverse, back, squares = pl.pallas_call(
         back_kernel,
         out_shape=(
-            jax.ShapeDtypeStruct((RANK, RANK), jnp.float32),
-            jax.ShapeDtypeStruct((width, RANK), jnp.float32),
+            pltpu.VMEM((RANK, RANK), jnp.float32),
+            pltpu.VMEM((width, RANK), jnp.float32),
             jax.ShapeDtypeStruct((16, 8, RANK), jnp.float32),
         ),
-    )(products)
+    )(pltpu.with_memory_space_constraint(products, pltpu.VMEM))
     basis = mm(proj, inverse, ((1,), (1,)))
     squares = jnp.sum(exchange(squares, ("y", "core")), axis=0)
+    new_momentum = buffer - feedback * mm(basis, back, ((1,), (1,)))
+    squares, new_momentum = lax.optimization_barrier((squares, new_momentum))
     squares = jnp.sum(exchange(copies(squares, 8), "z"), axis=(0, 1))
     right_next = back * lax.rsqrt(squares / FF + eps)
-    new_momentum = buffer - feedback * mm(basis, back, ((1,), (1,)))
     left_factor = basis * jnp.sqrt(jnp.float32(D))
     return (new_momentum, left_factor, right_next)
 

time: 139 us -> 134 us (0.964)
  blocking collectives: 99.8 us -> 108 us
  waiting for transfers between devices: 10.2 us -> 4.31 us
  starting transfers between devices: 9.65 us -> 6.14 us
  Pallas kernels: 9.39 us -> 7.59 us
    all_to_all x6 -> x7, blocking collectives: 93.3 us -> 102 us  [exchange(): return lax.all_to_all(parts, axis, 0, 0)]
    all_to_all x2 -> x1, waiting for transfers between devices: 10.2 us -> 4.31 us  [exchange(): return lax.all_to_all(parts, axis, 0, 0)]
    all_to_all x2 -> x1, starting transfers between devices: 9.65 us -> 6.14 us  [exchange(): return lax.all_to_all(parts, axis, 0, 0)]
    pallas_call x2, Pallas kernels: 9.39 us -> 7.59 us  [the longest x1 4.94 us: per_device(): pl.pallas_call(back_kernel, out_shape=(pltpu.VMEM((RANK, RANK), jnp.float...]
  transfers between devices with their start and end apart: 2 -> 1, of which waited for: 2 -> 1; matrix products, arithmetic and copies ran while one was open for 3% -> 3% of each run, Pallas kernels for 0% -> 0%
where the time goes in v4:
time: 134 us
  blocking collectives  108 us (81%)
  Pallas kernels  7.59 us (6%)
  starting transfers between devices  6.14 us (5%)
  matrix products  5.77 us (4%)
  waiting for transfers between devices  4.31 us (3%)
    all_to_all x7, blocking collectives, exchange(): return lax.all_to_all(parts, axis, 0, 0)  102 us
    all_gather x1, blocking collectives, sum_over_col(): return lax.all_gather(half, 'core', axis=0, tiled=True)  6.63 us
    all_to_all x1, starting transfers between devices, exchange(): return lax.all_to_all(parts, axis, 0, 0)  6.14 us
    dot_general x4, matrix products, mm(): lax.dot_general(a, b, (dims, ((), ())), precision=high, preferred_element...  5.77 us
    pallas_call x1, Pallas kernels, per_device(): pl.pallas_call(back_kernel, out_shape=(pltpu.VMEM((RANK, RANK), jnp.float...  4.94 us
    all_to_all x1, waiting for transfers between devices, exchange(): return lax.all_to_all(parts, axis, 0, 0)  4.31 us
  transfers between devices with their start and end apart: 1, of which 1 were waited for; matrix products, arithmetic and copies ran while one was open for 3% of the time, Pallas kernels for 0%

profile of v4, /device:TPU:1, one launch (start us, length us, event | category | flops | bytes accessed | tf_op | source)
XLA Modules:
  0.0 133.8 jit_solution(12132684307984254145)
XLA Ops:
  0.6 2.7 %shard_map.58 = f32[1280,128]{1,0:T(8,128)S(1)} custom-call(f32[208,1280]{1,0:T(8,128)} %bitcast.16, bf16[208,1280]{1,0:T(8,128)(2,1)} %bitcast.17, f32[208,128]{1,0:T(8,128)} %right_ref.1), custom_call_target="tpu_custom_call" | custom-call | tf_op jit(solution)/shard_map/pallas_call | solution.py:107
  3.3 18.0 %all_to_all.40 = f32[2,640,128]{2,1,0:T(8,128)S(1)} all-to-all(f32[2,640,128]{2,1,0:T(8,128)S(1)} %bitcast.14), channel_id=1, replica_groups=mesh['row'=8,'y'=8,'z'=8,'core'=2] {'core'}, dimensions={0} | all-to-all | bytes 1310720 | tf_op jit(solution)/shard_map/all_to_all | solution.py:23
  21.4 16.1 %all_to_all.41 = f32[8,80,128]{2,1,0:T(8,128)S(1)} all-to-all(f32[8,80,128]{2,1,0:T(8,128)S(1)} %bitcast.18), channel_id=1, replica_groups=mesh['row'=8,'y'=8,'z'=8,'core'=2] {'y'}, dimensions={0} | all-to-all | bytes 655360 | tf_op jit(solution)/shard_map/all_to_all | solution.py:23
  37.6 18.0 %all_to_all.42 = f32[8,80,128]{2,1,0:T(8,128)S(1)} all-to-all(f32[8,80,128]{2,1,0:T(8,128)S(1)} %broadcast_in_dim.8), channel_id=1, replica_groups=mesh['row'=8,'y'=8,'z'=8,'core'=2] {'z'}, dimensions={0} | all-to-all | bytes 655360 | tf_op jit(solution)/shard_map/all_to_all | solution.py:23
  55.6 12.4 %all_to_all.43 = f32[8,80,128]{2,1,0:T(8,128)S(1)} all-to-all(f32[8,80,128]{2,1,0:T(8,128)S(1)} %broadcast_in_dim.9), channel_id=1, replica_groups=mesh['row'=8,'y'=8,'z'=8,'core'=2] {'y'}, dimensions={0} | all-to-all | bytes 655360 | tf_op jit(solution)/shard_map/all_to_all | solution.py:23
  68.1 0.0 copy-start
  68.1 0.0 copy-start.1
  68.1 6.6 %all_gather.3 = f32[1280,128]{1,0:T(8,128)S(1)} all-gather(f32[640,128]{1,0:T(8,128)S(1)} %bitcast.19), channel_id=1, replica_groups=mesh['row'=8,'y'=8,'z'=8,'core'=2] {'core'}, dimensions={0}, use_global_device_ids=true | all-gather | bytes 983040 | tf_op jit(solution)/shard_map/all_gather | solution.py:36
  74.7 1.2 fusion.2
  75.9 0.0 copy-done
  75.9 0.0 copy-done.1
  76.0 1.0 fusion.1
  77.0 0.1 copy.7
  77.1 15.7 %all_to_all.44 = f32[8,16,336]{2,1,0:T(8,128)S(1)} all-to-all(f32[8,16,336]{2,1,0:T(8,128)S(1)} %bitcast.20), channel_id=1, replica_groups=mesh['row'=8,'y'=8,'z'=8,'core'=2] {'row'}, dimensions={0} | all-to-all | bytes 344064 | tf_op jit(solution)/shard_map/all_to_all | solution.py:23
  92.9 11.3 %all_to_all.45 = f32[8,16,336]{2,1,0:T(8,128)S(1)} all-to-all(f32[8,16,336]{2,1,0:T(8,128)S(1)} %broadcast_in_dim.10), channel_id=1, replica_groups=mesh['row'=8,'y'=8,'z'=8,'core'=2] {'row'}, dimensions={0} | all-to-all | bytes 344064 | tf_op jit(solution)/shard_map/all_to_all | solution.py:23
  104.2 4.9 %shard_map.59 = (f32[128,128]{1,0:T(8,128)S(1)}, f32[208,128]{1,0:T(8,128)S(1)}, f32[16,8,128]{2,1,0:T(8,128)}) custom-call(f32[128,336]{1,0:T(8,128)S(1)} %bitcast.15), custom_call_target="tpu_custom_call" | custom-call | tf_op jit(solution)/shard_map/pallas_call | solution.py:116
  109.1 6.1 %all-to-all-start.6 = ((f32[16,8,128]{2,1,0:T(8,128)}), f32[16,8,128]{2,1,0:T(8,128)S(1)}, u32[]{:S(2)}, u32[]{:S(2)}) async-start(f32[16,8,128]{2,1,0:T(8,128)} %get-tuple-element.8), calls=%async_computation.6 | async-start | bytes 131072 | tf_op jit(solution)/shard_map/all_to_all | solution.py:23
  115.3 1.5 %broadcast_multiply_fusion = (f32[1280,128]{1,0:T(8,128)}, f32[1280,128]{1,0:T(8,128)S(1)}) fusion(f32[1280,128]{1,0:T(8,128)S(1)} %all_gather.3, f32[128,128]{1,0:T(8,128)S(1)} %get-tuple-element.9), kind=kOutput, calls=%fused_computation.4 | convolution fusion | flops 251822080 | bytes 2031616 | tf_op jit(solution)/shard_map/dot_general | solution.py:19
  116.8 2.0 %fusion = f32[1280,208]{0,1:T(8,128)} fusion(f32[1280,128]{1,0:T(8,128)S(1)} %get-tuple-element.14, f32[208,128]{1,0:T(8,128)S(1)} %get-tuple-element.10, f32[1280,208]{0,1:T(8,128)S(1)} %copy-done, bf16[1280,208]{0,1:T(8,128)(2,1)S(1)} %copy-done.1), kind=kOutput, calls=%fused_computation.1 | convolution fusion | flops 410009600 | bytes 3424256 | tf_op jit(solution)/shard_map/dot_general | solution.py:19
  118.8 4.3 %all-to-all-done.6 = f32[16,8,128]{2,1,0:T(8,128)S(1)} async-done(((f32[16,8,128]{2,1,0:T(8,128)}), f32[16,8,128]{2,1,0:T(8,128)S(1)}, u32[]{:S(2)}, u32[]{:S(2)}) %all-to-all-start.6) | async-done | bytes 65568 | tf_op jit(solution)/shard_map/all_to_all | solution.py:23
  123.1 10.0 %all_to_all.46 = f32[8,8,128]{2,1,0:T(8,128)S(1)} all-to-all(f32[8,8,128]{2,1,0:T(8,128)S(1)} %broadcast_in_dim.11), channel_id=1, replica_groups=mesh['row'=8,'y'=8,'z'=8,'core'=2] {'z'}, dimensions={0} | all-to-all | bytes 65536 | tf_op jit(solution)/shard_map/all_to_all | solution.py:23
  133.1 0.7 broadcast_multiply_fusion.1
  (12 shorter events, 0.2 us)
Async XLA Ops:
  68.1 7.9 %copy-start = (f32[1280,208]{0,1:T(8,128)S(1)}, f32[1280,208]{0,1:T(8,128)}, u32[]{:S(2)}) copy-start(f32[1280,208]{0,1:T(8,128)} %param.3) | copy-start | bytes 3194884
  68.1 7.9 %copy-start.1 = (bf16[1280,208]{0,1:T(8,128)(2,1)S(1)}, bf16[1280,208]{0,1:T(8,128)(2,1)}, u32[]{:S(2)}) copy-start(bf16[1280,208]{0,1:T(8,128)(2,1)} %param.4) | copy-start | bytes 1597444
  109.1 14.0 %all-to-all-start.6 = ((f32[16,8,128]{2,1,0:T(8,128)}), f32[16,8,128]{2,1,0:T(8,128)S(1)}, u32[]{:S(2)}, u32[]{:S(2)}) async-start(f32[16,8,128]{2,1,0:T(8,128)} %get-tuple-element.8), calls=%async_computation.6 | async-start | bytes 131072 | tf_op jit(solution)/shard_map/all_to_all | solution.py:23

commit v5 on v4

--- a/solution.py
+++ b/solution.py
@@ -19,8 +19,16 @@
     return lax.dot_general(a, b, (dims, ((), ())), precision=high, preferred_element_type=jnp.float32)
 
 
-def exchange(parts, axis):
-    return lax.all_to_all(parts, axis, 0, 0)
+def lines(first, second):
+    along = {
+        "y": lambda core: [[(y * 8 + z) * 2 + core for y in range(8)] for z in range(8)],
+        "z": lambda core: [[(y * 8 + z) * 2 + core for z in range(8)] for y in range(8)],
+    }
+    return along[first](0) + along[second](1)
+
+
+def exchange(parts, axis, groups=None):
+    return lax.all_to_all(parts, axis, 0, 0, axis_index_groups=groups)
 
 
 def copies(x, n):
@@ -30,9 +38,10 @@
 def sum_over_col(partial):
     rows = partial.shape[0]
     half = jnp.sum(exchange(partial.reshape(2, rows // 2, RANK), "core"), axis=0)
-    share = jnp.sum(exchange(half.reshape(8, rows // 16, RANK), "y"), axis=0)
-    share = jnp.sum(exchange(copies(share, 8), "z"), axis=0)
-    half = exchange(copies(share, 8), "y").reshape(rows // 2, RANK)
+    one, other = lines("y", "z"), lines("z", "y")
+    share = jnp.sum(exchange(half.reshape(8, rows // 16, RANK), col, one), axis=0)
+    share = jnp.sum(exchange(copies(share, 8), col, other), axis=0)
+    half = exchange(copies(share, 8), col, one).reshape(rows // 2, RANK)
     return lax.all_gather(half, "core", axis=0, tiled=True)
 
 
@@ -90,7 +99,7 @@
     factor_inverse(products_ref, inverse_ref)
     back = mm(products_ref[:, RANK:].T, inverse_ref[...], ((1,), (1,)))
     back_ref[...] = back
-    squares = jnp.sum((back * back).reshape(-1, 8, RANK), axis=0)
+    squares = jnp.sum(back * back, axis=0, keepdims=True)
     for i in range(squares_ref.shape[0]):
         squares_ref[i] = squares
 
@@ -118,7 +127,7 @@
         out_shape=(
             pltpu.VMEM((RANK, RANK), jnp.float32),
             pltpu.VMEM((width, RANK), jnp.float32),
-            jax.ShapeDtypeStruct((16, 8, RANK), jnp.float32),
+            jax.ShapeDtypeStruct((16, 1, RANK), jnp.float32),
         ),
     )(pltpu.with_memory_space_constraint(products, pltpu.VMEM))
     basis = mm(proj, inverse, ((1,), (1,)))

time: 134 us -> 129 us (0.963)
  blocking collectives: 108 us -> 103 us
    all_to_all x7, blocking collectives: 102 us -> 97.1 us  [exchange(): return lax.all_to_all(parts, axis, 0, 0, axis_index_groups=groups)]
where the time goes in v5:
time: 129 us; the launch traced here: 128 us
  blocking collectives  103 us (80%)
  Pallas kernels  7.6 us (6%)
  starting transfers between devices  6.11 us (5%)
  matrix products  5.75 us (4%)
  waiting for transfers between devices  3.45 us (3%)
    all_to_all x7, blocking collectives, exchange(): return lax.all_to_all(parts, axis, 0, 0, axis_index_groups=groups)  97.1 us
    all_gather x1, blocking collectives, sum_over_col(): return lax.all_gather(half, 'core', axis=0, tiled=True)  6.4 us
    all_to_all x1, starting transfers between devices, exchange(): return lax.all_to_all(parts, axis, 0, 0, axis_index_groups=groups)  6.11 us
    dot_general x4, matrix products, mm(): lax.dot_general(a, b, (dims, ((), ())), precision=high, preferred_element...  5.75 us
    pallas_call x1, Pallas kernels, per_device(): pl.pallas_call(back_kernel, out_shape=(pltpu.VMEM((RANK, RANK), jnp.float...  4.95 us
    all_to_all x1, waiting for transfers between devices, exchange(): return lax.all_to_all(parts, axis, 0, 0, axis_index_groups=groups)  3.45 us
    pallas_call x1, Pallas kernels, per_device(): pl.pallas_call(proj_kernel, out_shape=pltpu.VMEM((rows, RANK), jnp.float32))  2.65 us
  transfers between devices with their start and end apart: 1, of which 1 were waited for; matrix products, arithmetic and copies ran while one was open for 3% of the time, Pallas kernels for 0%

profile of v5, /device:TPU:1, one launch (start us, length us, event | category | flops | bytes accessed | tf_op | source)
XLA Modules:
  0.0 128.1 jit_solution(11575566450289787032)
XLA Ops:
  0.6 2.7 %shard_map.58 = f32[1280,128]{1,0:T(8,128)S(1)} custom-call(f32[208,1280]{1,0:T(8,128)} %bitcast.19, bf16[208,1280]{1,0:T(8,128)(2,1)} %bitcast.20, f32[208,128]{1,0:T(8,128)} %right_ref.1), custom_call_target="tpu_custom_call" | custom-call | tf_op jit(solution)/shard_map/pallas_call | solution.py:116
  3.3 18.0 %all_to_all.40 = f32[2,640,128]{2,1,0:T(8,128)S(1)} all-to-all(f32[2,640,128]{2,1,0:T(8,128)S(1)} %bitcast.17), channel_id=1, replica_groups=mesh['row'=8,'y'=8,'z'=8,'core'=2] {'core'}, dimensions={0} | all-to-all | bytes 1310720 | tf_op jit(solution)/shard_map/all_to_all | solution.py:31
  21.4 13.6 %all_to_all.41 = f32[8,80,128]{2,1,0:T(8,128)S(1)} all-to-all(f32[8,80,128]{2,1,0:T(8,128)S(1)} %bitcast.21), channel_id=1, replica_groups={{0,16,32,48,64,80,96,112},{2,18,34,50,66,82,98,114},{4,20,36,52,68,84,1..., dimensions={0} | all-to-all | bytes 655360 | tf_op jit(solution)/shard_map/all_to_all | solution.py:31
  35.0 17.1 %all_to_all.42 = f32[8,80,128]{2,1,0:T(8,128)S(1)} all-to-all(f32[8,80,128]{2,1,0:T(8,128)S(1)} %broadcast_in_dim.10), channel_id=1, replica_groups={{0,2,4,6,8,10,12,14},{16,18,20,22,24,26,28,30},{32,34,36,38,40,42,44,46..., dimensions={0} | all-to-all | bytes 655360 | tf_op jit(solution)/shard_map/all_to_all | solution.py:31
  52.2 12.4 %all_to_all.43 = f32[8,80,128]{2,1,0:T(8,128)S(1)} all-to-all(f32[8,80,128]{2,1,0:T(8,128)S(1)} %broadcast_in_dim.11), channel_id=1, replica_groups={{0,16,32,48,64,80,96,112},{2,18,34,50,66,82,98,114},{4,20,36,52,68,84,1..., dimensions={0} | all-to-all | bytes 655360 | tf_op jit(solution)/shard_map/all_to_all | solution.py:31
  64.6 0.0 copy-start
  64.6 0.0 copy-start.1
  64.6 6.4 %all_gather.3 = f32[1280,128]{1,0:T(8,128)S(1)} all-gather(f32[640,128]{1,0:T(8,128)S(1)} %bitcast.22), channel_id=1, replica_groups=mesh['row'=8,'y'=8,'z'=8,'core'=2] {'core'}, dimensions={0}, use_global_device_ids=true | all-gather | bytes 983040 | tf_op jit(solution)/shard_map/all_gather | solution.py:45
  71.0 1.2 fusion.2
  72.2 0.0 copy-done
  72.2 0.0 copy-done.1
  72.2 1.0 fusion.1
  73.3 0.1 copy.8
  73.4 15.7 %all_to_all.44 = f32[8,16,336]{2,1,0:T(8,128)S(1)} all-to-all(f32[8,16,336]{2,1,0:T(8,128)S(1)} %bitcast.23), channel_id=1, replica_groups=mesh['row'=8,'y'=8,'z'=8,'core'=2] {'row'}, dimensions={0} | all-to-all | bytes 344064 | tf_op jit(solution)/shard_map/all_to_all | solution.py:31
  89.1 11.3 %all_to_all.45 = f32[8,16,336]{2,1,0:T(8,128)S(1)} all-to-all(f32[8,16,336]{2,1,0:T(8,128)S(1)} %broadcast_in_dim.12), channel_id=1, replica_groups=mesh['row'=8,'y'=8,'z'=8,'core'=2] {'row'}, dimensions={0} | all-to-all | bytes 344064 | tf_op jit(solution)/shard_map/all_to_all | solution.py:31
  100.5 5.0 %shard_map.59 = (f32[128,128]{1,0:T(8,128)S(1)}, f32[208,128]{1,0:T(8,128)S(1)}, f32[16,1,128]{2,1,0:T(1,128)}) custom-call(f32[128,336]{1,0:T(8,128)S(1)} %bitcast.18), custom_call_target="tpu_custom_call" | custom-call | tf_op jit(solution)/shard_map/pallas_call | solution.py:125
  105.4 6.1 %all-to-all-start.6 = ((f32[16,1,128]{2,1,0:T(1,128)}), f32[16,1,128]{2,1,0:T(1,128)S(1)}, u32[]{:S(2)}, u32[]{:S(2)}) async-start(f32[16,1,128]{2,1,0:T(1,128)} %get-tuple-element.8), calls=%async_computation.6 | async-start | bytes 16384 | tf_op jit(solution)/shard_map/all_to_all | solution.py:31
  111.5 1.5 %broadcast_multiply_fusion = (f32[1280,128]{1,0:T(8,128)}, f32[1280,128]{1,0:T(8,128)S(1)}) fusion(f32[1280,128]{1,0:T(8,128)S(1)} %all_gather.3, f32[128,128]{1,0:T(8,128)S(1)} %get-tuple-element.9), kind=kOutput, calls=%fused_computation.4 | convolution fusion | flops 251822080 | bytes 2031616 | tf_op jit(solution)/shard_map/dot_general | solution.py:19
  113.0 2.0 %fusion = f32[1280,208]{0,1:T(8,128)} fusion(f32[1280,128]{1,0:T(8,128)S(1)} %get-tuple-element.14, f32[208,128]{1,0:T(8,128)S(1)} %get-tuple-element.10, f32[1280,208]{0,1:T(8,128)S(1)} %copy-done, bf16[1280,208]{0,1:T(8,128)(2,1)S(1)} %copy-done.1), kind=kOutput, calls=%fused_computation.1 | convolution fusion | flops 410009600 | bytes 3424256 | tf_op jit(solution)/shard_map/dot_general | solution.py:19
  115.0 3.5 %all-to-all-done.6 = f32[16,1,128]{2,1,0:T(1,128)S(1)} async-done(((f32[16,1,128]{2,1,0:T(1,128)}), f32[16,1,128]{2,1,0:T(1,128)S(1)}, u32[]{:S(2)}, u32[]{:S(2)}) %all-to-all-start.6) | async-done | bytes 8224 | tf_op jit(solution)/shard_map/all_to_all | solution.py:31
  118.5 8.9 %all_to_all.46 = f32[8,1,128]{2,1,0:T(1,128)S(1)} all-to-all(f32[8,1,128]{2,1,0:T(1,128)S(1)} %broadcast_in_dim.14), channel_id=1, replica_groups=mesh['row'=8,'y'=8,'z'=8,'core'=2] {'z'}, dimensions={0} | all-to-all | bytes 8192 | tf_op jit(solution)/shard_map/all_to_all | solution.py:31
  127.5 0.7 broadcast_multiply_fusion.1
  (12 shorter events, 0.2 us)
Async XLA Ops:
  64.6 7.6 %copy-start = (f32[1280,208]{0,1:T(8,128)S(1)}, f32[1280,208]{0,1:T(8,128)}, u32[]{:S(2)}) copy-start(f32[1280,208]{0,1:T(8,128)} %param.3) | copy-start | bytes 3194884
  64.6 7.6 %copy-start.1 = (bf16[1280,208]{0,1:T(8,128)(2,1)S(1)}, bf16[1280,208]{0,1:T(8,128)(2,1)}, u32[]{:S(2)}) copy-start(bf16[1280,208]{0,1:T(8,128)(2,1)} %param.4) | copy-start | bytes 1597444
  105.4 13.1 %all-to-all-start.6 = ((f32[16,1,128]{2,1,0:T(1,128)}), f32[16,1,128]{2,1,0:T(1,128)S(1)}, u32[]{:S(2)}, u32[]{:S(2)}) async-start(f32[16,1,128]{2,1,0:T(1,128)} %get-tuple-element.8), calls=%async_computation.6 | async-start | bytes 16384 | tf_op jit(solution)/shard_map/all_to_all | solution.py:31

commit v6 on v5

--- a/solution.py
+++ b/solution.py
@@ -111,33 +111,58 @@
         out_ref[part, :] = mm(buffer, right_ref[...], ((0,), (0,)))
 
 
+def products_kernel(proj_ref, momentum_ref, grad_ref, out_ref):
+    proj = proj_ref[...]
+    buffer = momentum_ref[...] + grad_ref[...].astype(jnp.float32)
+    out_ref[:, :RANK] = mm(proj, proj, ((0,), (0,)))
+    out_ref[:, RANK:] = mm(buffer, proj, ((1,), (0,))).T
+
+
+def outputs_kernel(proj_ref, inverse_ref, back_ref, momentum_ref, grad_ref, left_ref, feedback_ref):
+    basis = mm(proj_ref[...], inverse_ref[...], ((1,), (1,)))
+    left_ref[...] = basis * D**0.5
+    buffer = momentum_ref[...] + grad_ref[...].astype(jnp.float32)
+    feedback_ref[...] = buffer - feedback * mm(back_ref[...], basis, ((1,), (1,)))
+
+
+def in_vmem(x):
+    return pltpu.with_memory_space_constraint(x, pltpu.VMEM)
+
+
 def per_device(momentum, grad, right_prev):
     rows, width = momentum.shape
     partial = pl.pallas_call(
         proj_kernel, out_shape=pltpu.VMEM((rows, RANK), jnp.float32)
     )(momentum.T, grad.T, right_prev)
     proj = sum_over_col(partial)
-    buffer = momentum + grad.astype(jnp.float32)
-    products = jnp.concatenate(
-        [mm(proj, proj, ((0,), (0,))), mm(proj, buffer, ((0,), (0,)))], axis=1
-    )
+    momentum_t, grad_t, proj = in_vmem(momentum.T), in_vmem(grad.T), in_vmem(proj)
+    products = pl.pallas_call(
+        products_kernel, out_shape=pltpu.VMEM((RANK, RANK + width), jnp.float32)
+    )(proj, momentum_t, grad_t)
     products = sum_over_row(products)
     inverse, back, squares = pl.pallas_call(
         back_kernel,
         out_shape=(
             pltpu.VMEM((RANK, RANK), jnp.float32),
             pltpu.VMEM((width, RANK), jnp.float32),
-            jax.ShapeDtypeStruct((16, 1, RANK), jnp.float32),
+            jax.ShapeDtypeStruct((128, 1, RANK), jnp.float32),
         ),
-    )(pltpu.with_memory_space_constraint(products, pltpu.VMEM))
-    basis = mm(proj, inverse, ((1,), (1,)))
-    squares = jnp.sum(exchange(squares, ("y", "core")), axis=0)
-    new_momentum = buffer - feedback * mm(basis, back, ((1,), (1,)))
-    squares, new_momentum = lax.optimization_barrier((squares, new_momentum))
-    squares = jnp.sum(exchange(copies(squares, 8), "z"), axis=(0, 1))
+    )(in_vmem(products))
+    squares = jnp.sum(exchange(squares, col), axis=(0, 1))
+    left_factor, new_momentum = pl.pallas_call(
+        outputs_kernel,
+        out_shape=(
+            jax.ShapeDtypeStruct((rows, RANK), jnp.float32),
+            jax.ShapeDtypeStruct((width, rows), jnp.float32),
+        ),
+        cost_estimate=pl.CostEstimate(
+            flops=12 * rows * RANK * (RANK + width),
+            bytes_accessed=4 * rows * (RANK + 2 * width),
+            transcendentals=0,
+        ),
+    )(proj, in_vmem(inverse), in_vmem(back), momentum_t, grad_t)
     right_next = back * lax.rsqrt(squares / FF + eps)
-    left_factor = basis * jnp.sqrt(jnp.float32(D))
-    return (new_momentum, left_factor, right_next)
+    return (new_momentum.T, left_factor, right_next)
 
 
 def solution(mesh):

time: 129 us -> 126 us (0.977)
  blocking collectives: 103 us -> 94.6 us
  matrix products: 5.75 us -> 0 us
  Pallas kernels: 7.6 us -> 12.8 us
  waiting for transfers between devices: 3.45 us -> 8.13 us
  starting transfers between devices: 6.11 us -> 8.01 us
    all_to_all x7 -> x6, blocking collectives: 97.1 us -> 88.3 us  [exchange(): return lax.all_to_all(parts, axis, 0, 0, axis_index_groups=groups)]
    dot_general x4 -> x0, matrix products: 5.75 us -> none  [mm(): lax.dot_general(a, b, (dims, ((), ())), precision=high, preferred_element...]
    pallas_call x0 -> x2, Pallas kernels: none -> 5.17 us  [the longest x1 3.48 us: per_device(): pl.pallas_call(outputs_kernel, out_shape=(jax.ShapeDtypeStruct((rows, RAN...]
    all_to_all x1, waiting for transfers between devices: 3.45 us -> 8.13 us  [exchange(): return lax.all_to_all(parts, axis, 0, 0, axis_index_groups=groups)]
    all_to_all x1, starting transfers between devices: 6.11 us -> 8.01 us  [exchange(): return lax.all_to_all(parts, axis, 0, 0, axis_index_groups=groups)]
  transfers between devices with their start and end apart: 1 -> 1, of which waited for: 1 -> 1; matrix products, arithmetic and copies ran while one was open for 3% -> 0% of each run, Pallas kernels for 0% -> 3%
where the time goes in v6:
time: 126 us; the launch traced here: 125 us
  blocking collectives  94.6 us (75%)
  Pallas kernels  12.8 us (10%)
  waiting for transfers between devices  8.13 us (6%)
  starting transfers between devices  8.01 us (6%)
    all_to_all x6, blocking collectives, exchange(): return lax.all_to_all(parts, axis, 0, 0, axis_index_groups=groups)  88.3 us
    all_to_all x1, waiting for transfers between devices, exchange(): return lax.all_to_all(parts, axis, 0, 0, axis_index_groups=groups)  8.13 us
    all_to_all x1, starting transfers between devices, exchange(): return lax.all_to_all(parts, axis, 0, 0, axis_index_groups=groups)  8.01 us
    all_gather x1, blocking collectives, sum_over_col(): return lax.all_gather(half, 'core', axis=0, tiled=True)  6.27 us
    pallas_call x1, Pallas kernels, per_device(): pl.pallas_call(back_kernel, out_shape=(pltpu.VMEM((RANK, RANK), jnp.float...  4.99 us
    pallas_call x1, Pallas kernels, per_device(): pl.pallas_call(outputs_kernel, out_shape=(jax.ShapeDtypeStruct((rows, RAN...  3.48 us
    pallas_call x1, Pallas kernels, per_device(): pl.pallas_call(proj_kernel, out_shape=pltpu.VMEM((rows, RANK), jnp.float32))  2.65 us
  transfers between devices with their start and end apart: 1, of which 1 were waited for; matrix products, arithmetic and copies ran while one was open for 0% of the time, Pallas kernels for 3%

profile of v6, /device:TPU:1, one launch (start us, length us, event | category | flops | bytes accessed | tf_op | source)
XLA Modules:
  0.0 125.2 jit_solution(6078730793296682516)
XLA Ops:
  0.6 2.7 %shard_map.58 = f32[1280,128]{1,0:T(8,128)S(1)} custom-call(f32[208,1280]{1,0:T(8,128)} %bitcast.8, bf16[208,1280]{1,0:T(8,128)(2,1)} %bitcast.12, f32[208,128]{1,0:T(8,128)} %right_ref.1), custom_call_target="tpu_custom_call" | custom-call | tf_op jit(solution)/shard_map/pallas_call | solution.py:134
  3.3 18.0 %all_to_all.35 = f32[2,640,128]{2,1,0:T(8,128)S(1)} all-to-all(f32[2,640,128]{2,1,0:T(8,128)S(1)} %bitcast.11), channel_id=1, replica_groups=mesh['row'=8,'y'=8,'z'=8,'core'=2] {'core'}, dimensions={0} | all-to-all | bytes 1310720 | tf_op jit(solution)/shard_map/all_to_all | solution.py:31
  21.4 13.6 %all_to_all.36 = f32[8,80,128]{2,1,0:T(8,128)S(1)} all-to-all(f32[8,80,128]{2,1,0:T(8,128)S(1)} %bitcast.17), channel_id=1, replica_groups={{0,16,32,48,64,80,96,112},{2,18,34,50,66,82,98,114},{4,20,36,52,68,84,1..., dimensions={0} | all-to-all | bytes 655360 | tf_op jit(solution)/shard_map/all_to_all | solution.py:31
  35.0 17.1 %all_to_all.37 = f32[8,80,128]{2,1,0:T(8,128)S(1)} all-to-all(f32[8,80,128]{2,1,0:T(8,128)S(1)} %broadcast_in_dim.6), channel_id=1, replica_groups={{0,2,4,6,8,10,12,14},{16,18,20,22,24,26,28,30},{32,34,36,38,40,42,44,46..., dimensions={0} | all-to-all | bytes 655360 | tf_op jit(solution)/shard_map/all_to_all | solution.py:31
  52.1 0.0 copy-start
  52.2 0.0 copy-start.1
  52.2 12.5 %all_to_all.38 = f32[8,80,128]{2,1,0:T(8,128)S(1)} all-to-all(f32[8,80,128]{2,1,0:T(8,128)S(1)} %broadcast_in_dim.7), channel_id=1, replica_groups={{0,16,32,48,64,80,96,112},{2,18,34,50,66,82,98,114},{4,20,36,52,68,84,1..., dimensions={0} | all-to-all | bytes 655360 | tf_op jit(solution)/shard_map/all_to_all | solution.py:31
  64.7 6.3 %all_gather.3.proj_ref = f32[1280,128]{1,0:T(8,128)S(1)} all-gather(f32[640,128]{1,0:T(8,128)S(1)} %bitcast.18), channel_id=1, replica_groups=mesh['row'=8,'y'=8,'z'=8,'core'=2] {'core'}, dimensions={0}, use_global_device_ids=true | all-gather | bytes 983040 | tf_op jit(solution)/shard_map/all_gather | solution.py:45
  71.0 0.0 copy-done
  71.0 0.0 copy-done.1
  71.0 1.7 %shard_map.59 = f32[128,336]{1,0:T(8,128)S(1)} custom-call(f32[1280,128]{1,0:T(8,128)S(1)} %all_gather.3.proj_ref, f32[208,1280]{1,0:T(8,128)S(1)} %bitcast.9, bf16[208,1280]{1,0:T(8,128)(2,1)S(1)} %bitcast.13), custom_call_target="tpu_custom_call" | custom-call | tf_op jit(solution)/shard_map/pallas_call | solution.py:139
  72.7 15.7 %all_to_all.39 = f32[8,16,336]{2,1,0:T(8,128)S(1)} all-to-all(f32[8,16,336]{2,1,0:T(8,128)S(1)} %bitcast.15), channel_id=1, replica_groups=mesh['row'=8,'y'=8,'z'=8,'core'=2] {'row'}, dimensions={0} | all-to-all | bytes 344064 | tf_op jit(solution)/shard_map/all_to_all | solution.py:31
  88.5 11.3 %all_to_all.40 = f32[8,16,336]{2,1,0:T(8,128)S(1)} all-to-all(f32[8,16,336]{2,1,0:T(8,128)S(1)} %broadcast_in_dim.8), channel_id=1, replica_groups=mesh['row'=8,'y'=8,'z'=8,'core'=2] {'row'}, dimensions={0} | all-to-all | bytes 344064 | tf_op jit(solution)/shard_map/all_to_all | solution.py:31
  99.8 5.0 %shard_map.60 = (f32[128,128]{1,0:T(8,128)S(1)}, f32[208,128]{1,0:T(8,128)S(1)}, f32[128,1,128]{2,1,0:T(1,128)}) custom-call(f32[128,336]{1,0:T(8,128)S(1)} %bitcast.16), custom_call_target="tpu_custom_call" | custom-call | tf_op jit(solution)/shard_map/pallas_call | solution.py:143
  104.8 8.0 %all-to-all-start.6 = ((f32[128,1,128]{2,1,0:T(1,128)}), f32[128,1,128]{2,1,0:T(1,128)S(1)}, u32[]{:S(2)}, u32[]{:S(2)}) async-start(f32[128,1,128]{2,1,0:T(1,128)} %get-tuple-element.12), calls=%async_computation.6 | async-start | bytes 131072 | tf_op jit(solution)/shard_map/all_to_all | solution.py:31
  112.8 3.5 %shard_map.61 = (f32[1280,128]{1,0:T(8,128)}, f32[208,1280]{1,0:T(8,128)}) custom-call(f32[1280,128]{1,0:T(8,128)S(1)} %all_gather.3.proj_ref, f32[128,128]{1,0:T(8,128)S(1)} %get-tuple-element.8.inverse_ref, f32[208,128]{1,0:T(8,128)S(1)} %get-tuple-element.9.back_ref, f32[208,1280]{1,0:T(8,128)S(1)} %bitcast.10, bf16[208,1280]{1,0:T(8,128)(2,1)S(1)} %bitcast.14), custom_call_target="tpu_custom_call" | custom-call | flops 660602880 | bytes 2785280 | tf_op jit(solution)/shard_map/pallas_call | solution.py:152
  116.3 8.1 %all-to-all-done.6 = f32[128,1,128]{2,1,0:T(1,128)S(1)} async-done(((f32[128,1,128]{2,1,0:T(1,128)}), f32[128,1,128]{2,1,0:T(1,128)S(1)}, u32[]{:S(2)}, u32[]{:S(2)}) %all-to-all-start.6) | async-done | bytes 65568 | tf_op jit(solution)/shard_map/all_to_all | solution.py:31
  124.4 0.2 reduce_sum.49
  124.6 0.7 broadcast_multiply_fusion
  (8 shorter events, 0.2 us)
Async XLA Ops:
  52.1 18.9 %copy-start = (f32[1280,208]{0,1:T(8,128)S(1)}, f32[1280,208]{0,1:T(8,128)}, u32[]{:S(2)}) copy-start(f32[1280,208]{0,1:T(8,128)} %param.3) | copy-start | bytes 3194884
  52.2 18.9 %copy-start.1 = (bf16[1280,208]{0,1:T(8,128)(2,1)S(1)}, bf16[1280,208]{0,1:T(8,128)(2,1)}, u32[]{:S(2)}) copy-start(bf16[1280,208]{0,1:T(8,128)(2,1)} %param.4) | copy-start | bytes 1597444
  104.8 19.6 %all-to-all-start.6 = ((f32[128,1,128]{2,1,0:T(1,128)}), f32[128,1,128]{2,1,0:T(1,128)S(1)}, u32[]{:S(2)}, u32[]{:S(2)}) async-start(f32[128,1,128]{2,1,0:T(1,128)} %get-tuple-element.12), calls=%async_computation.6 | async-start | bytes 131072 | tf_op jit(solution)/shard_map/all_to_all | solution.py:31

commit v7 on v6

--- a/solution.py
+++ b/solution.py
@@ -35,9 +35,9 @@
     return jnp.broadcast_to(x[None], (n,) + x.shape)
 
 
-def sum_over_col(partial):
-    rows = partial.shape[0]
-    half = jnp.sum(exchange(partial.reshape(2, rows // 2, RANK), "core"), axis=0)
+def sum_over_col(away, own):
+    rows = 2 * own.shape[0]
+    half = own + lax.ppermute(away, "core", [(0, 1), (1, 0)])
     one, other = lines("y", "z"), lines("z", "y")
     share = jnp.sum(exchange(half.reshape(8, rows // 16, RANK), col, one), axis=0)
     share = jnp.sum(exchange(copies(share, 8), col, other), axis=0)
@@ -104,11 +104,12 @@
         squares_ref[i] = squares
 
 
-def proj_kernel(momentum_ref, grad_ref, right_ref, out_ref):
-    for i in range(out_ref.shape[0] // 256):
-        part = slice(256 * i, 256 * i + 256)
+def proj_kernel(core_ref, momentum_ref, grad_ref, right_ref, away_ref, own_ref):
+    rows = own_ref.shape[0]
+    for ref, side in ((away_ref, 1 - core_ref[0]), (own_ref, core_ref[0])):
+        part = pl.ds(pl.multiple_of(side * rows, rows), rows)
         buffer = momentum_ref[:, part] + grad_ref[:, part].astype(jnp.float32)
-        out_ref[part, :] = mm(buffer, right_ref[...], ((0,), (0,)))
+        ref[...] = mm(buffer, right_ref[...], ((0,), (0,)))
 
 
 def products_kernel(proj_ref, momentum_ref, grad_ref, out_ref):
@@ -131,10 +132,13 @@
 
 def per_device(momentum, grad, right_prev):
     rows, width = momentum.shape
-    partial = pl.pallas_call(
-        proj_kernel, out_shape=pltpu.VMEM((rows, RANK), jnp.float32)
-    )(momentum.T, grad.T, right_prev)
-    proj = sum_over_col(partial)
+    vmem = pl.BlockSpec(memory_space=pltpu.VMEM)
+    away, own = pl.pallas_call(
+        proj_kernel,
+        out_shape=(pltpu.VMEM((rows // 2, RANK), jnp.float32),) * 2,
+        in_specs=[pl.BlockSpec(memory_space=pltpu.SMEM), vmem, vmem, vmem],
+    )(lax.axis_index("core").reshape(1), momentum.T, grad.T, right_prev)
+    proj = sum_over_col(away, own)
     momentum_t, grad_t, proj = in_vmem(momentum.T), in_vmem(grad.T), in_vmem(proj)
     products = pl.pallas_call(
         products_kernel, out_shape=pltpu.VMEM((RANK, RANK + width), jnp.float32)
@@ -145,7 +149,7 @@
         out_shape=(
             pltpu.VMEM((RANK, RANK), jnp.float32),
             pltpu.VMEM((width, RANK), jnp.float32),
-            jax.ShapeDtypeStruct((128, 1, RANK), jnp.float32),
+            pltpu.VMEM((128, 1, RANK), jnp.float32),
         ),
     )(in_vmem(products))
     squares = jnp.sum(exchange(squares, col), axis=(0, 1))

time: 126 us -> 125 us (level)
  blocking collectives: 94.6 us -> 76.5 us
  starting transfers between devices: 8.01 us -> 24 us
    all_to_all x6 -> x5, blocking collectives: 88.3 us -> 70.3 us  [exchange(): return lax.all_to_all(parts, axis, 0, 0, axis_index_groups=groups)]
    ppermute x0 -> x1, starting transfers between devices: none -> 16.1 us  [sum_over_col(): half = own + lax.ppermute(away, 'core', [(0, 1), (1, 0)])]
  transfers between devices with their start and end apart: 1 -> 2, of which waited for: 1 -> 2; matrix products, arithmetic and copies ran while one was open for 0% -> 0% of each run, Pallas kernels for 3% -> 3%
where the time goes in v7:
time: 125 us
  blocking collectives  76.5 us (61%)
  starting transfers between devices  24 us (19%)
  Pallas kernels  13.1 us (10%)
  waiting for transfers between devices  9.36 us (7%)
    all_to_all x5, blocking collectives, exchange(): return lax.all_to_all(parts, axis, 0, 0, axis_index_groups=groups)  70.3 us
    ppermute x1, starting transfers between devices, sum_over_col(): half = own + lax.ppermute(away, 'core', [(0, 1), (1, 0)])  16.1 us
    all_to_all x1, waiting for transfers between devices, exchange(): return lax.all_to_all(parts, axis, 0, 0, axis_index_groups=groups)  8.13 us
    all_to_all x1, starting transfers between devices, exchange(): return lax.all_to_all(parts, axis, 0, 0, axis_index_groups=groups)  7.98 us
    all_gather x1, blocking collectives, sum_over_col(): return lax.all_gather(half, 'core', axis=0, tiled=True)  6.27 us
    pallas_call x1, Pallas kernels, per_device(): pl.pallas_call(back_kernel, out_shape=(pltpu.VMEM((RANK, RANK), jnp.float...  5 us
    pallas_call x1, Pallas kernels, per_device(): pl.pallas_call(outputs_kernel, out_shape=(jax.ShapeDtypeStruct((rows, RAN...  3.49 us
    pallas_call x1, Pallas kernels, per_device(): pl.pallas_call(proj_kernel, out_shape=(pltpu.VMEM((rows // 2, RANK), jnp....  2.89 us
  transfers between devices with their start and end apart: 2, of which 2 were waited for; matrix products, arithmetic and copies ran while one was open for 0% of the time, Pallas kernels for 3%

profile of v7, /device:TPU:1, one launch (start us, length us, event | category | flops | bytes accessed | tf_op | source)
XLA Modules:
  0.0 124.7 jit_solution(12705695424810047938)
XLA Ops:
  0.6 2.9 %shard_map.58 = (f32[640,128]{1,0:T(8,128)S(1)}, f32[640,128]{1,0:T(8,128)S(1)}) custom-call(s32[1]{0:T(128)} %bitcast.core_ref, f32[208,1280]{1,0:T(8,128)} %bitcast.8, bf16[208,1280]{1,0:T(8,128)(2,1)} %bitcast.11, f32[208,128]{1,0:T(8,128)} %right_ref.1), custom_call_target="tpu_custom_call" | custom-call | tf_op jit(solution)/shard_map/pallas_call | solution.py:136
  3.5 16.1 %collective-permute-start = (f32[640,128]{1,0:T(8,128)S(1)}, f32[640,128]{1,0:T(8,128)S(1)}, u32[]{:S(2)}, u32[]{:S(2)}) collective-permute-start(f32[640,128]{1,0:T(8,128)S(1)} %get-tuple-element.11), channel_id=1, source_target_pairs={{0,1},{1,0},{2,3},{3,2},{4,5},{5,4},{6,7},{7,6},{8,9},{9,8},{10,11... | collective-permute-start | bytes 983048 | tf_op jit(solution)/shard_map/ppermute | solution.py:40
  19.6 1.2 collective-permute-done
  20.9 13.6 %all_to_all.30 = f32[8,80,128]{2,1,0:T(8,128)S(1)} all-to-all(f32[8,80,128]{2,1,0:T(8,128)S(1)} %bitcast.16), channel_id=1, replica_groups={{0,16,32,48,64,80,96,112},{2,18,34,50,66,82,98,114},{4,20,36,52,68,84,1..., dimensions={0} | all-to-all | bytes 655360 | tf_op jit(solution)/shard_map/all_to_all | solution.py:31
  34.5 17.1 %all_to_all.31 = f32[8,80,128]{2,1,0:T(8,128)S(1)} all-to-all(f32[8,80,128]{2,1,0:T(8,128)S(1)} %broadcast_in_dim.6), channel_id=1, replica_groups={{0,2,4,6,8,10,12,14},{16,18,20,22,24,26,28,30},{32,34,36,38,40,42,44,46..., dimensions={0} | all-to-all | bytes 655360 | tf_op jit(solution)/shard_map/all_to_all | solution.py:31
  51.7 0.0 copy-start
  51.7 0.0 copy-start.1
  51.7 12.5 %all_to_all.32 = f32[8,80,128]{2,1,0:T(8,128)S(1)} all-to-all(f32[8,80,128]{2,1,0:T(8,128)S(1)} %broadcast_in_dim.7), channel_id=1, replica_groups={{0,16,32,48,64,80,96,112},{2,18,34,50,66,82,98,114},{4,20,36,52,68,84,1..., dimensions={0} | all-to-all | bytes 655360 | tf_op jit(solution)/shard_map/all_to_all | solution.py:31
  64.3 6.3 %all_gather.3.proj_ref = f32[1280,128]{1,0:T(8,128)S(1)} all-gather(f32[640,128]{1,0:T(8,128)S(1)} %bitcast.17), channel_id=1, replica_groups=mesh['row'=8,'y'=8,'z'=8,'core'=2] {'core'}, dimensions={0}, use_global_device_ids=true | all-gather | bytes 983040 | tf_op jit(solution)/shard_map/all_gather | solution.py:45
  70.5 0.0 copy-done
  70.5 0.0 copy-done.1
  70.5 1.7 %shard_map.59 = f32[128,336]{1,0:T(8,128)S(1)} custom-call(f32[1280,128]{1,0:T(8,128)S(1)} %all_gather.3.proj_ref, f32[208,1280]{1,0:T(8,128)S(1)} %bitcast.9, bf16[208,1280]{1,0:T(8,128)(2,1)S(1)} %bitcast.12), custom_call_target="tpu_custom_call" | custom-call | tf_op jit(solution)/shard_map/pallas_call | solution.py:143
  72.3 15.7 %all_to_all.33 = f32[8,16,336]{2,1,0:T(8,128)S(1)} all-to-all(f32[8,16,336]{2,1,0:T(8,128)S(1)} %bitcast.14), channel_id=1, replica_groups=mesh['row'=8,'y'=8,'z'=8,'core'=2] {'row'}, dimensions={0} | all-to-all | bytes 344064 | tf_op jit(solution)/shard_map/all_to_all | solution.py:31
  88.0 11.3 %all_to_all.34 = f32[8,16,336]{2,1,0:T(8,128)S(1)} all-to-all(f32[8,16,336]{2,1,0:T(8,128)S(1)} %broadcast_in_dim.8), channel_id=1, replica_groups=mesh['row'=8,'y'=8,'z'=8,'core'=2] {'row'}, dimensions={0} | all-to-all | bytes 344064 | tf_op jit(solution)/shard_map/all_to_all | solution.py:31
  99.3 5.0 %shard_map.60 = (f32[128,128]{1,0:T(8,128)S(1)}, f32[208,128]{1,0:T(8,128)S(1)}, f32[128,1,128]{2,1,0:T(1,128)}) custom-call(f32[128,336]{1,0:T(8,128)S(1)} %bitcast.15), custom_call_target="tpu_custom_call" | custom-call | tf_op jit(solution)/shard_map/pallas_call | solution.py:147
  104.3 8.0 %all-to-all-start.5 = ((f32[128,1,128]{2,1,0:T(1,128)}), f32[128,1,128]{2,1,0:T(1,128)S(1)}, u32[]{:S(2)}, u32[]{:S(2)}) async-start(f32[128,1,128]{2,1,0:T(1,128)} %get-tuple-element.16), calls=%async_computation.5 | async-start | bytes 131072 | tf_op jit(solution)/shard_map/all_to_all | solution.py:31
  112.3 3.5 %shard_map.61 = (f32[1280,128]{1,0:T(8,128)}, f32[208,1280]{1,0:T(8,128)}) custom-call(f32[1280,128]{1,0:T(8,128)S(1)} %all_gather.3.proj_ref, f32[128,128]{1,0:T(8,128)S(1)} %get-tuple-element.12.inverse_ref, f32[208,128]{1,0:T(8,128)S(1)} %get-tuple-element.13.back_ref, f32[208,1280]{1,0:T(8,128)S(1)} %bitcast.10, bf16[208,1280]{1,0:T(8,128)(2,1)S(1)} %bitcast.13), custom_call_target="tpu_custom_call" | custom-call | flops 660602880 | bytes 2785280 | tf_op jit(solution)/shard_map/pallas_call | solution.py:156
  115.8 8.1 %all-to-all-done.5 = f32[128,1,128]{2,1,0:T(1,128)S(1)} async-done(((f32[128,1,128]{2,1,0:T(1,128)}), f32[128,1,128]{2,1,0:T(1,128)S(1)}, u32[]{:S(2)}, u32[]{:S(2)}) %all-to-all-start.5) | async-done | bytes 65568 | tf_op jit(solution)/shard_map/all_to_all | solution.py:31
  123.9 0.2 reduce_sum.39
  124.1 0.7 broadcast_multiply_fusion
  (8 shorter events, 0.2 us)
Async XLA Ops:
  3.5 17.3 %collective-permute-start = (f32[640,128]{1,0:T(8,128)S(1)}, f32[640,128]{1,0:T(8,128)S(1)}, u32[]{:S(2)}, u32[]{:S(2)}) collective-permute-start(f32[640,128]{1,0:T(8,128)S(1)} %get-tuple-element.11), channel_id=1, source_target_pairs={{0,1},{1,0},{2,3},{3,2},{4,5},{5,4},{6,7},{7,6},{8,9},{9,8},{10,11... | collective-permute-start | bytes 983048 | tf_op jit(solution)/shard_map/ppermute | solution.py:40
  51.7 18.9 %copy-start = (f32[1280,208]{0,1:T(8,128)S(1)}, f32[1280,208]{0,1:T(8,128)}, u32[]{:S(2)}) copy-start(f32[1280,208]{0,1:T(8,128)} %param.3) | copy-start | bytes 3194884
  51.7 18.9 %copy-start.1 = (bf16[1280,208]{0,1:T(8,128)(2,1)S(1)}, bf16[1280,208]{0,1:T(8,128)(2,1)}, u32[]{:S(2)}) copy-start(bf16[1280,208]{0,1:T(8,128)(2,1)} %param.4) | copy-start | bytes 1597444
  104.3 19.6 %all-to-all-start.5 = ((f32[128,1,128]{2,1,0:T(1,128)}), f32[128,1,128]{2,1,0:T(1,128)S(1)}, u32[]{:S(2)}, u32[]{:S(2)}) async-start(f32[128,1,128]{2,1,0:T(1,128)} %get-tuple-element.16), calls=%async_computation.5 | async-start | bytes 131072 | tf_op jit(solution)/shard_map/all_to_all | solution.py:31
